TPU v7x, 512 devices: a whole 4x8x8 slice. The times are simulated.
512 devices in a mesh: tm: 8 (over y), bl: 32 (over x, z_lo, core), chan: 2 (over z_hi).
Axes of the slice: x: 4, y: 8, z: 8 (z_hi: 2, z_lo: 4; z = z_hi * 4 + z_lo), core: 2. Of those that a mesh axis runs over, the one named last changes fastest.
Arguments:
- model: bfloat16 [8, 4, 8, 8, 8192], P('tm', 'chan', None, None, 'bl'), may hold values from -2.5 to 2.5
- vis: float32 [8, 4, 8, 8192], P('tm', 'chan', None, 'bl'), may hold values from -6 to 6
- weights: float32 [8, 4, 8192], P('tm', 'chan', 'bl'), may hold values from 0.2 to 4
- antenna1: int32 [8192], P('bl'), may hold values from 0 to 511, as said below
- antenna2: int32 [8192], P('bl'), may hold values from 0 to 511
- live: int32 [8192], P('bl'), may hold values from 0 to 1, as said below
- gains: float32 [2, 8, 8, 512], P('chan', None, None, 'bl'), may hold values from -3 to 3
Outputs:
- gains_out: float32 [2, 8, 8, 512], P('chan', None, None, 'bl')
- whitened: float32 [2, 8, 8, 512], P('chan', None, None, 'bl')
Inputs may be any that keep to these rules, and one draw needn't show every extreme that they name: antenna1 and antenna2 differ on every baseline. `live`: padded slots are marked 0.
All inputs are finite; a program needn't handle non-finite values.
Results may differ from a plain program's by a relative error of at most 0.0003.
Values sent between devices are 32-bit elements; how exact they have to be, the bound alone decides.
No kernel may reach another device: no remote copies, remote signals or barrier semaphores. Data moves between devices by JAX's collectives and lax.ppermute only.
A program may use at most 64 MiB of HBM per device.

v0:
```python
import jax
import jax.numpy as jnp
from jax import lax
from jax.sharding import PartitionSpec as P

ITERS = 3


step_scale = 0.8


def jones(array):
    return [(array[..., index, :], array[..., index + 4, :]) for index in range(4)]


def cmul(left, right):
    return (left[0] * right[0] - left[1] * right[1], left[0] * right[1] + left[1] * right[0])


def cadd(left, right):
    return (left[0] + right[0], left[1] + right[1])


def adjoint(matrix):
    return [(entry[0], -entry[1]) for entry in (matrix[0], matrix[2], matrix[1], matrix[3])]


def product(left, right):
    result = []
    for row in range(2):
        for col in range(2):
            result.append(
                cadd(cmul(left[2 * row], right[col]), cmul(left[2 * row + 1], right[2 + col]))
            )
    return result


def stack_jones(matrix):
    return jnp.stack([entry[0] for entry in matrix] + [entry[1] for entry in matrix], axis=-2)


def norm_sq(matrix):
    return sum((entry[0] * entry[0] + entry[1] * entry[1] for entry in matrix))


def baseline_terms(near, far, model, vis, weight):
    near_j = jones(near)
    far_j = jones(far)
    model_j = jones(model)
    right_a = product(model_j, adjoint(far_j))
    left_b = product(near_j, model_j)
    each = product(near_j, right_a)
    observed = jones(vis[..., None, :, :])
    scale = weight[..., None, :]
    resid = []
    for index in range(4):
        pred_re = jnp.sum(each[index][0], axis=-2, keepdims=True)
        pred_im = jnp.sum(each[index][1], axis=-2, keepdims=True)
        resid.append(
            (scale * (observed[index][0] - pred_re), scale * (observed[index][1] - pred_im))
        )
    term_p = -stack_jones(product(resid, adjoint(right_a)))
    term_q = -stack_jones(product(adjoint(resid), left_b))
    curv_p = scale * norm_sq(right_a)
    curv_q = scale * norm_sq(left_b)
    return (term_p, term_q, curv_p, curv_q)


def fetch_gains(local):
    return lax.all_gather(local, "bl", axis=2, tiled=True)


def station_partials(full, model_f, vis_loc, weight_loc, antenna1, antenna2):
    dirs = full.shape[0]
    stations = full.shape[2]
    base = antenna1.shape[0]
    near = jnp.take(full, antenna1, axis=2)
    far = jnp.take(full, antenna2, axis=2)
    term_p, term_q, curv_p, curv_q = baseline_terms(near, far, model_f, vis_loc, weight_loc)
    flat_p = jnp.concatenate(
        [jnp.sum(term_p, axis=0).reshape(dirs * 8, base), jnp.sum(curv_p, axis=0)], axis=0
    )
    flat_q = jnp.concatenate(
        [jnp.sum(term_q, axis=0).reshape(dirs * 8, base), jnp.sum(curv_q, axis=0)], axis=0
    )
    station = (
        jax.ops.segment_sum(flat_p.T, antenna1, num_segments=stations)
        + jax.ops.segment_sum(flat_q.T, antenna2, num_segments=stations)
    ).T
    return (station[: dirs * 8], station[dirs * 8 :])


def per_device(model, vis, weights, antenna1, antenna2, live, gains):
    local = gains[0]
    dirs = local.shape[0]
    owned = local.shape[2]
    model_f = model[0].astype(jnp.float32)
    vis_loc = vis[0]
    weight_loc = weights[0] * live.astype(jnp.float32)[None, :]
    white = jnp.zeros_like(local)
    for step in range(ITERS):
        full = fetch_gains(local)
        grad_all, curv_all = station_partials(
            full, model_f, vis_loc, weight_loc, antenna1, antenna2
        )
        grad_own, curv_own = (
            lax.psum_scatter(grad_all, "bl", scatter_dimension=1, tiled=True),
            lax.psum_scatter(curv_all, "bl", scatter_dimension=1, tiled=True),
        )
        grad_own, curv_own = lax.psum((grad_own, curv_own), "tm")
        grad_loc = grad_own.reshape(dirs, 8, owned)
        denom = curv_own[:, None, :] + 1.0
        white = grad_loc / jnp.sqrt(denom)
        local = local - step_scale * grad_loc / denom
    return (local[None], white[None])


def solution(mesh):
    return jax.shard_map(
        per_device,
        mesh=mesh,
        in_specs=(
            P("tm", "chan", None, None, "bl"),
            P("tm", "chan", None, "bl"),
            P("tm", "chan", "bl"),
            P("bl"),
            P("bl"),
            P("bl"),
            P("chan", None, None, "bl"),
        ),
        out_specs=(P("chan", None, None, "bl"), P("chan", None, None, "bl")),
        check_vma=False,
    )
```

profile of v0, /device:TPU:1, one launch (start us, length us, event | category | flops | bytes accessed | tf_op | source)
XLA Modules:
  0.0 1198.9 jit_solution(632926921417399512)
XLA Ops:
  7.2 0.7 compare_select_fusion
  7.9 0.7 compare_and_fusion
  8.6 0.7 compare_select_fusion.1
  9.3 0.7 compare_and_fusion.1
  10.0 0.8 copy.319
  10.8 59.0 %all-gather = f32[1,8,8,512]{2,1,0,3:T(8,128)S(1)} all-gather(f32[1,8,8,16]{2,1,0,3:T(8,128)S(1)} %copy.319), channel_id=2, replica_groups=mesh['tm'=8,'bl'=32,'chan'=2] {'bl'}, dimensions={3}, use_global_device_ids=true | all-gather | bytes 135168 | tf_op jit(solution)/shard_map/all_gather | solution.py:70
  70.4 1.0 gather_fusion.1
  72.6 1.0 gather_fusion
  74.0 4.2 fusion.239
  78.2 1.6 copy.329
  79.7 1.6 copy.328
  81.3 1.6 copy.327
  82.9 1.6 copy.326
  84.5 1.5 copy.325
  87.2 0.7 copy.394
  88.0 0.8 add_reduce_fusion.19
  89.4 1.6 scatter_custom_fusion
  91.2 1.6 scatter_custom_fusion.1
  92.9 0.8 slice_bitcast_fusion.4
  93.8 0.7 slice_bitcast_fusion.5
  94.6 140.1 %reduce-scatter.21.cloned.1.call-done = f32[16,8]{1,0:T(8,128)} async-done(((f32[512,8]{1,0:T(8,128)}), f32[16,8]{1,0:T(8,128)}) %reduce-scatter.21.cloned.1.call-update) | async-done | bytes 528
  234.7 0.8 copy.371
  235.5 145.2 %reduce-scatter.19.cloned.1.call-done = f32[16,64]{1,0:T(8,128)} async-done(((f32[512,64]{1,0:T(8,128)}), f32[16,64]{1,0:T(8,128)}) %reduce-scatter.19.cloned.1.call-update) | async-done | bytes 4112
  380.7 0.8 copy.369
  381.4 22.1 %all-reduce.2 = (f32[64,16]{1,0:T(8,128)S(1)}, f32[8,16]{1,0:T(8,128)S(1)}) all-reduce(f32[64,16]{1,0:T(8,128)S(1)} %copy.369, f32[8,16]{1,0:T(8,128)S(1)} %copy.371), channel_id=1, replica_groups=mesh['tm'=8,'bl'=32,'chan'=2] {'tm'}, use_global_device_ids=true, to_apply=%region_15.17 | all-reduce | flops 1152 | bytes 9216 | tf_op jit(solution)/shard_map/psum | solution.py:110
  403.7 64.1 %all_gather.10 = f32[8,8,512]{1,0,2:T(8,128)S(1)} all-gather(f32[8,8,16]{1,0,2:T(8,128)S(1)} %copy.336), channel_id=1, replica_groups=mesh['tm'=8,'bl'=32,'chan'=2] {'bl'}, dimensions={2}, use_global_device_ids=true | all-gather | bytes 135168 | tf_op jit(solution)/shard_map/all_gather | solution.py:70
  467.9 2.1 gather_fusion.3
  470.0 1.2 gather_fusion.2
  471.2 1.5 copy.338
  474.4 4.2 fusion.238
  478.6 1.5 copy.345
  480.1 1.6 copy.344
  481.7 1.6 copy.343
  483.2 1.6 copy.342
  484.8 1.6 copy.341
  488.3 1.6 scatter_custom_fusion.2
  490.2 1.6 scatter_custom_fusion.3
  491.8 0.8 slice_bitcast_fusion.2
  492.7 0.7 slice_bitcast_fusion.3
  493.5 134.9 %reduce-scatter.25.cloned.1.call-done = f32[16,8]{1,0:T(8,128)} async-done(((f32[512,8]{1,0:T(8,128)}), f32[16,8]{1,0:T(8,128)}) %reduce-scatter.25.cloned.1.call-update) | async-done | bytes 528
  628.4 0.8 copy.375
  629.2 145.0 %reduce-scatter.23.cloned.1.call-done = f32[16,64]{1,0:T(8,128)} async-done(((f32[512,64]{1,0:T(8,128)}), f32[16,64]{1,0:T(8,128)}) %reduce-scatter.23.cloned.1.call-update) | async-done | bytes 4112
  774.2 0.8 copy.373
  775.0 22.1 %all-reduce.1 = (f32[64,16]{1,0:T(8,128)S(1)}, f32[8,16]{1,0:T(8,128)S(1)}) all-reduce(f32[64,16]{1,0:T(8,128)S(1)} %copy.373, f32[8,16]{1,0:T(8,128)S(1)} %copy.375), channel_id=1, replica_groups=mesh['tm'=8,'bl'=32,'chan'=2] {'tm'}, use_global_device_ids=true, to_apply=%region_33.35 | all-reduce | flops 1152 | bytes 9216 | tf_op jit(solution)/shard_map/psum | solution.py:110
  797.3 64.2 %all_gather.11 = f32[8,8,512]{1,0,2:T(8,128)S(1)} all-gather(f32[8,8,16]{1,0,2:T(8,128)S(1)} %copy.352), channel_id=1, replica_groups=mesh['tm'=8,'bl'=32,'chan'=2] {'bl'}, dimensions={2}, use_global_device_ids=true | all-gather | bytes 135168 | tf_op jit(solution)/shard_map/all_gather | solution.py:70
  861.4 2.1 gather_fusion.5
  863.6 1.2 gather_fusion.4
  864.8 1.5 copy.354
  868.0 4.2 fusion.237
  872.2 1.5 copy.361
  873.7 1.6 copy.360
  875.3 1.6 copy.359
  876.8 1.6 copy.358
  878.4 1.6 copy.357
  882.6 1.6 scatter_custom_fusion.4
  884.4 1.6 scatter_custom_fusion.5
  886.1 0.8 slice_bitcast_fusion
  887.0 0.7 slice_bitcast_fusion.1
  887.7 134.9 %reduce-scatter.29.cloned.1.call-done = f32[16,8]{1,0:T(8,128)} async-done(((f32[512,8]{1,0:T(8,128)}), f32[16,8]{1,0:T(8,128)}) %reduce-scatter.29.cloned.1.call-update) | async-done | bytes 528
  1022.6 0.8 copy.379
  1023.4 145.0 %reduce-scatter.27.cloned.1.call-done = f32[16,64]{1,0:T(8,128)} async-done(((f32[512,64]{1,0:T(8,128)}), f32[16,64]{1,0:T(8,128)}) %reduce-scatter.27.cloned.1.call-update) | async-done | bytes 4112
  1168.4 0.8 copy.377
  1169.2 22.2 %all-reduce = (f32[1,8,8,16]{3,2,1,0:T(8,128)S(1)}, f32[8,16]{1,0:T(8,128)S(1)}) all-reduce(f32[1,8,8,16]{3,2,1,0:T(8,128)S(1)} %bitcast.1283, f32[8,16]{1,0:T(8,128)S(1)} %copy.379), channel_id=1, replica_groups=mesh['tm'=8,'bl'=32,'chan'=2] {'tm'}, use_global_device_ids=true, to_apply=%region_51.53 | all-reduce | flops 1152 | bytes 9216 | tf_op jit(solution)/shard_map/psum | solution.py:110
  1191.4 0.7 broadcast_divide_fusion
  (177 shorter events, 12.3 us)
Async XLA Ops:
  7.2 64.7 %copy-start.1 = (bf16[1,2,8,8,256]{4,3,2,1,0:T(8,128)(2,1)S(1)}, bf16[1,2,8,8,256]{4,3,2,1,0:T(8,128)(2,1)}, u32[]{:S(2)}) copy-start(bf16[1,2,8,8,256]{4,3,2,1,0:T(8,128)(2,1)} %param.9) | copy-start | bytes 196612
  7.2 227.5 %reduce-scatter.21.cloned.1.call-start = ((), (), s32[]{:S(2)}) async-start(), calls=%async_computation.7 | async-start | bytes 270336
  8.6 63.3 %copy-start.19 = (pred[256]{0:T(512)(128)(4,1)}, pred[256]{0:T(512)(128)(4,1)S(1)}, u32[]{:S(2)}) copy-start(pred[256]{0:T(512)(128)(4,1)S(1)} %compare_and_fusion) | copy-start | bytes 772
  10.0 63.6 %copy-start.16 = (pred[256]{0:T(512)(128)(4,1)}, pred[256]{0:T(512)(128)(4,1)S(1)}, u32[]{:S(2)}) copy-start(pred[256]{0:T(512)(128)(4,1)S(1)} %compare_and_fusion.1) | copy-start | bytes 772
  69.8 0.6 copy-start.15
  69.8 4.1 copy-start.14
  78.2 6.2 copy-start.22
  84.4 403.3 %copy-start.13 = (f32[256]{0:T(256)}, f32[256]{0:T(256)S(1)}, u32[]{:S(2)}) copy-start(f32[256]{0:T(256)S(1)} %convert_element_type.9) | copy-start | bytes 3076
  84.4 3.5 copy-start.12
  89.3 314.3 %copy-start = (f32[1,8,8,16]{3,2,1,0:T(8,128)S(1)}, f32[1,8,8,16]{3,2,1,0:T(8,128)}, u32[]{:S(2)}) copy-start(f32[1,8,8,16]{3,2,1,0:T(8,128)} %param.15) | copy-start | bytes 12292
  93.8 286.9 %reduce-scatter.19.cloned.1.call-start = ((), (), s32[]{:S(2)}) async-start(), calls=%async_computation.6 | async-start | bytes 270336
  94.5 378.2 %copy-start.20 = (pred[256]{0:T(512)(128)(4,1)S(1)}, pred[256]{0:T(512)(128)(4,1)}, u32[]{:S(2)}) copy-start(pred[256]{0:T(512)(128)(4,1)} %copy-done.19) | copy-start | bytes 772
  94.5 533.9 %reduce-scatter.25.cloned.1.call-start = ((), (), s32[]{:S(2)}) async-start(), calls=%async_computation.9 | async-start | bytes 270336
  403.7 70.3 %copy-start.17 = (pred[256]{0:T(512)(128)(4,1)S(1)}, pred[256]{0:T(512)(128)(4,1)}, u32[]{:S(2)}) copy-start(pred[256]{0:T(512)(128)(4,1)} %copy-done.16) | copy-start | bytes 772
  486.8 0.9 copy-start.5
  486.8 0.9 copy-start.9
  486.8 0.9 copy-start.10
  486.8 0.9 copy-start.11
  492.7 281.5 %reduce-scatter.23.cloned.1.call-start = ((), (), s32[]{:S(2)}) async-start(), calls=%async_computation.8 | async-start | bytes 270336
  493.5 372.9 %copy-start.21 = (pred[256]{0:T(512)(128)(4,1)S(1)}, pred[256]{0:T(512)(128)(4,1)}, u32[]{:S(2)}) copy-start(pred[256]{0:T(512)(128)(4,1)} %copy-done.19) | copy-start | bytes 772
  493.5 529.2 %reduce-scatter.29.cloned.1.call-start = ((), (), s32[]{:S(2)}) async-start(), calls=%async_computation.11 | async-start | bytes 270336
  797.3 70.4 %copy-start.18 = (pred[256]{0:T(512)(128)(4,1)S(1)}, pred[256]{0:T(512)(128)(4,1)}, u32[]{:S(2)}) copy-start(pred[256]{0:T(512)(128)(4,1)} %copy-done.16) | copy-start | bytes 772
  880.4 0.9 copy-start.2
  880.4 0.9 copy-start.3
  880.4 0.9 copy-start.4
  880.4 0.9 copy-start.6
  880.4 0.9 copy-start.7
  880.4 0.9 copy-start.8
  886.9 281.5 %reduce-scatter.27.cloned.1.call-start = ((), (), s32[]{:S(2)}) async-start(), calls=%async_computation.10 | async-start | bytes 270336
Sparse Core Ops, SparseCore 0:
  93.9 140.7 reduce-scatter.20
  237.7 142.8 reduce-scatter.18
  492.8 135.5 reduce-scatter.24
  631.3 142.8 reduce-scatter.22
  887.1 135.5 reduce-scatter.28
  1025.5 142.8 reduce-scatter.26
where the time goes:
time: 1210 us; the launch traced here: 1200 us
  waiting for transfers between devices  845 us (70%)
  blocking collectives  254 us (21%)
  local copies, waits for them, and re-layouts  64 us (5%)
  other arithmetic  20.5 us (2%)
  between operations  15.1 us (1%)
    unnamed x12, waiting for transfers between devices  845 us
    all_gather x3, blocking collectives, fetch_gains(): return lax.all_gather(local, 'bl', axis=2, tiled=True)  187 us
    psum x3, blocking collectives, per_device(): grad_own, curv_own = lax.psum((grad_own, curv_own), 'tm')  66.4 us
    slice x15, local copies, waits for them, and re-layouts, jones(): array[..., index, :]  24.4 us
  transfers between devices with their start and end apart: 6, of which 6 were waited for; matrix products, arithmetic and copies ran while one was open for 0% of the time, Pallas kernels for 0%

commit v1 on v0

v1 whole, which is shorter than its diff:
```python
import functools

import jax
import jax.numpy as jnp
from jax import lax
from jax.experimental import pallas as pl
from jax.experimental.pallas import tpu as pltpu
from jax.sharding import Mesh
from jax.sharding import PartitionSpec as P

ITERS = 3
STEP = 0.8
DIRS = 8
COMPS = 8
VALS = DIRS * COMPS
LANES = 128
RUN = LANES // DIRS


def cmul(left, right):
    return (left[0] * right[0] - left[1] * right[1], left[0] * right[1] + left[1] * right[0])


def cadd(left, right):
    return (left[0] + right[0], left[1] + right[1])


def adjoint(matrix):
    return [(entry[0], -entry[1]) for entry in (matrix[0], matrix[2], matrix[1], matrix[3])]


def product(left, right):
    result = []
    for row in range(2):
        for col in range(2):
            result.append(
                cadd(cmul(left[2 * row], right[col]), cmul(left[2 * row + 1], right[2 + col]))
            )
    return result


def norm_sq(matrix):
    return sum(entry[0] * entry[0] + entry[1] * entry[1] for entry in matrix)


def halves(value):
    high = value.astype(jnp.bfloat16)
    low = (value - high.astype(jnp.float32)).astype(jnp.bfloat16)
    return high, low


def select_sum(left, right, dims):
    total = None
    for part in halves(left):
        term = lax.dot_general(
            part, right, (dims, ((), ())), preferred_element_type=jnp.float32
        )
        total = term if total is None else total + term
    return total


def pick_sum(left, right, dims):
    total = None
    for part in halves(right):
        term = lax.dot_general(
            left, part, (dims, ((), ())), preferred_element_type=jnp.float32
        )
        total = term if total is None else total + term
    return total


def partials_kernel(
    gains_ref, model_ref, vis_ref, weight_ref, live_ref, first_ref, second_ref,
    out_ref, picked_ref, model_f_ref, terms_ref,
):
    base = first_ref.shape[1]
    pairs = gains_ref.shape[0]
    channels = model_ref.shape[0]
    station = jnp.concatenate([first_ref[...], second_ref[...]], axis=1)
    rows = lax.broadcasted_iota(jnp.int32, (pairs, 2 * base), 0)
    hot = jnp.where(rows == station // 2, 1.0, 0.0).astype(jnp.bfloat16)
    odd = station % 2 == 1

    both = select_sum(gains_ref[...].T, hot, ((1,), (0,)))
    picked = jnp.where(odd, both[VALS:], both[:VALS])
    cuts = base // LANES
    for cut in range(2 * cuts):
        picked_ref[cut] = picked[:, cut * LANES : (cut + 1) * LANES]

    def entries(ref, at):
        comps = [ref[at, pl.ds(c, DIRS, stride=COMPS), :] for c in range(COMPS)]
        return [(comps[i], comps[i + 4]) for i in range(4)]

    live = live_ref[...].astype(jnp.float32)
    curvs = [None] * (2 * cuts)
    for cut in range(cuts):
        lanes = slice(cut * LANES, (cut + 1) * LANES)
        near = entries(picked_ref, cut)
        far = entries(picked_ref, cuts + cut)
        totals = None
        for channel in range(channels):
            model_f_ref[0] = model_ref[channel, :, lanes].astype(jnp.float32)
            model = entries(model_f_ref, 0)
            scale = weight_ref[channel : channel + 1, lanes] * live[:, lanes]
            right_a = product(model, adjoint(far))
            left_b = product(near, model)
            each = product(near, right_a)
            vis = vis_ref[channel, :, lanes]
            resid = []
            for index in range(4):
                pred_re = jnp.sum(each[index][0], axis=0, keepdims=True)
                pred_im = jnp.sum(each[index][1], axis=0, keepdims=True)
                resid.append(
                    (
                        scale * (vis[index : index + 1] - pred_re),
                        scale * (vis[index + 4 : index + 5] - pred_im),
                    )
                )
            new = (
                product(resid, adjoint(right_a)),
                product(adjoint(resid), left_b),
                scale * norm_sq(right_a),
                scale * norm_sq(left_b),
            )
            totals = new if totals is None else jax.tree.map(lambda a, b: a + b, totals, new)
        for side in range(2):
            at = side * cuts + cut
            for index, (real, imag) in enumerate(totals[side]):
                terms_ref[at, pl.ds(index, DIRS, stride=COMPS), :] = -real
                terms_ref[at, pl.ds(index + 4, DIRS, stride=COMPS), :] = -imag
            curvs[at] = totals[2 + side]

    terms = jnp.concatenate([terms_ref[at] for at in range(2 * cuts)], axis=1)
    curv = jnp.concatenate(curvs, axis=1)
    spread = jnp.concatenate([jnp.where(odd, 0.0, terms), jnp.where(odd, terms, 0.0)], axis=0)
    grads = pick_sum(hot, spread, ((1,), (1,)))
    place = station % RUN
    spread = jnp.concatenate([jnp.where(place == j, curv, 0.0) for j in range(RUN)], axis=0)
    rows = lax.broadcasted_iota(jnp.int32, (2 * pairs // RUN, 2 * base), 0)
    hot = jnp.where(rows == station // RUN, 1.0, 0.0).astype(jnp.bfloat16)
    curvs = pick_sum(hot, spread, ((1,), (1,)))
    for peer in range(pairs // RUN):
        at = peer * (RUN + 2)
        out_ref[at : at + RUN, :] = grads[peer * RUN : (peer + 1) * RUN]
        out_ref[at + RUN : at + RUN + 2, :] = curvs[2 * peer : 2 * peer + 2]


def partials(gains, model, vis, weights, live, first, second):
    pairs = gains.shape[0]
    base = first.shape[1]
    return pl.pallas_call(
        partials_kernel,
        out_shape=jax.ShapeDtypeStruct((pairs // RUN * (RUN + 2), LANES), jnp.float32),
        in_specs=[pl.BlockSpec(memory_space=pltpu.VMEM)] * 7,
        out_specs=pl.BlockSpec(memory_space=pltpu.VMEM),
        scratch_shapes=[
            pltpu.VMEM((2 * base // LANES, VALS, LANES), jnp.float32),
            pltpu.VMEM((1, VALS, LANES), jnp.float32),
            pltpu.VMEM((2 * base // LANES, VALS, LANES), jnp.float32),
        ],
        compiler_params=pltpu.CompilerParams(vmem_limit_bytes=16 * 2**20),
        name="partials",
    )(gains, model, vis, weights, live, first, second)


def peers_sum(parts_ref, rows):
    total = parts_ref[0:rows, :]
    for at in range(rows, parts_ref.shape[0], rows):
        total = total + parts_ref[at : at + rows, :]
    return total


def total_kernel(parts_ref, copies_ref):
    rows = RUN + 2
    total = peers_sum(parts_ref, rows)
    for at in range(0, copies_ref.shape[0], rows):
        copies_ref[at : at + rows, :] = total


def total(parts, peers):
    return pl.pallas_call(
        total_kernel,
        out_shape=jax.ShapeDtypeStruct((peers * (RUN + 2), LANES), jnp.float32),
        in_specs=[pl.BlockSpec(memory_space=pltpu.VMEM)],
        out_specs=pl.BlockSpec(memory_space=pltpu.VMEM),
        compiler_params=pltpu.CompilerParams(vmem_limit_bytes=16 * 2**20),
        name="total",
    )(parts)


def stepped(at_ref, parts_ref, gains_ref):
    sums = peers_sum(parts_ref, RUN + 2)
    grad = sums[:RUN]
    row = lax.broadcasted_iota(jnp.int32, (RUN, LANES), 0)
    lane = lax.broadcasted_iota(jnp.int32, (RUN, LANES), 1)
    curv = jnp.where(row < RUN // 2, sums[RUN : RUN + 1], sums[RUN + 1 : RUN + 2])
    curv = jnp.where(lane // (2 * DIRS) == row % (RUN // 2), curv, 0.0)
    source = lax.broadcasted_iota(jnp.int32, (LANES, LANES), 0)
    target = lax.broadcasted_iota(jnp.int32, (LANES, LANES), 1)
    wide = jnp.where(source % (2 * DIRS) == target // COMPS, 1.0, 0.0)
    denom = 1.0 + jnp.dot(
        curv, wide, precision=lax.Precision.HIGHEST, preferred_element_type=jnp.float32
    )
    old = gains_ref[pl.ds(pl.multiple_of(at_ref[0], RUN), RUN), :]
    return old - STEP * grad / denom, grad / jnp.sqrt(denom)


def step_kernel(at_ref, parts_ref, gains_ref, copies_ref):
    gains, _ = stepped(at_ref, parts_ref, gains_ref)
    for at in range(0, copies_ref.shape[0], RUN):
        copies_ref[at : at + RUN, :] = gains


def last_kernel(at_ref, parts_ref, gains_ref, gains_out_ref, white_ref, rows_ref):
    half = RUN // 2
    source = lax.broadcasted_iota(jnp.int32, (half, RUN), 0)
    target = lax.broadcasted_iota(jnp.int32, (half, RUN), 1)
    for value, out_ref in zip(stepped(at_ref, parts_ref, gains_ref), (gains_out_ref, white_ref)):
        rows_ref[...] = value
        turned = rows_ref[pl.ds(pl.multiple_of(at_ref[1], half), half), :].T
        out = None
        for odd in range(2):
            place = jnp.where(target == 2 * source + odd, 1.0, 0.0)
            part = jnp.dot(
                turned[odd * VALS : (odd + 1) * VALS],
                place,
                precision=lax.Precision.HIGHEST,
                preferred_element_type=jnp.float32,
            )
            out = part if out is None else out + part
        out_ref[...] = out


def step(at, parts, gains, peers):
    return pl.pallas_call(
        step_kernel,
        out_shape=jax.ShapeDtypeStruct((peers * RUN, LANES), jnp.float32),
        in_specs=[pl.BlockSpec(memory_space=pltpu.SMEM)]
        + [pl.BlockSpec(memory_space=pltpu.VMEM)] * 2,
        out_specs=pl.BlockSpec(memory_space=pltpu.VMEM),
        compiler_params=pltpu.CompilerParams(vmem_limit_bytes=16 * 2**20),
        name="step",
    )(at, parts, gains)


def last(at, parts, gains):
    return pl.pallas_call(
        last_kernel,
        out_shape=(jax.ShapeDtypeStruct((VALS, RUN), jnp.float32),) * 2,
        in_specs=[pl.BlockSpec(memory_space=pltpu.SMEM)]
        + [pl.BlockSpec(memory_space=pltpu.VMEM)] * 2,
        out_specs=(pl.BlockSpec(memory_space=pltpu.VMEM),) * 2,
        scratch_shapes=[pltpu.VMEM((RUN, LANES), jnp.float32)],
        compiler_params=pltpu.CompilerParams(vmem_limit_bytes=16 * 2**20),
        name="last",
    )(at, parts, gains)


def exchange(rows, axes, peers):
    count = rows.shape[0]
    sent = rows.reshape(peers, 1, count // peers * LANES)
    return lax.all_to_all(sent, axes, 0, 0).reshape(count, LANES)


def per_device(model, vis, weights, antenna1, antenna2, live, gains):
    base = antenna1.shape[0]
    channels = model.shape[1]
    owned = gains.shape[3]
    chips, others = ("x", "z"), ("y", "core")
    model = model.reshape(channels, VALS, base)
    vis, weights = vis[0], weights[0]
    first, second, live = (a.reshape(1, base) for a in (antenna1, antenna2, live))
    mine = gains.reshape(VALS, owned).T.reshape(1, owned * VALS // LANES, LANES)
    mine = jnp.broadcast_to(mine, (32,) + mine.shape[1:]).reshape(-1, LANES)
    full = exchange(mine, ("x", "z", "core"), 32)
    chip = lax.axis_index("x") * 4 + lax.axis_index("z")
    at = jnp.stack([chip * RUN, lax.axis_index("core") * (RUN // 2)]).astype(jnp.int32)
    for turn in range(ITERS):
        sent = partials(full, model, vis, weights, live, first, second)
        sent = total(exchange(sent, chips, 16), 16)
        sums = exchange(sent, others, 16)
        if turn < ITERS - 1:
            full = exchange(step(at, sums, full, 16), chips, 16)
    return tuple(out.reshape(gains.shape) for out in last(at, sums, full))


def solution(mesh):
    fine = Mesh(mesh.devices.reshape(8, 4, 4, 2, 2), ("y", "x", "z", "core", "chan"))
    bl = ("x", "z", "core")
    return jax.shard_map(
        per_device,
        mesh=fine,
        in_specs=(
            P("y", "chan", None, None, bl),
            P("y", "chan", None, bl),
            P("y", "chan", bl),
            P(bl),
            P(bl),
            P(bl),
            P("chan", None, None, bl),
        ),
        out_specs=(P("chan", None, None, bl), P("chan", None, None, bl)),
        check_vma=False,
    )
```

time: 1210 us -> 129 us (0.11)
  waiting for transfers between devices: 845 us -> 9.25 us
  blocking collectives: 254 us -> 100 us
  local copies, waits for them, and re-layouts: 64 us -> 1.68 us
  other arithmetic: 20.5 us -> 0.07 us
  between operations: 15.1 us -> 0.71 us
    unnamed x12 -> x0, waiting for transfers between devices: 845 us -> none
    all_gather x3 -> x0, blocking collectives: 187 us -> none  [fetch_gains(): return lax.all_gather(local, 'bl', axis=2, tiled=True)]
    all_to_all x0 -> x8, blocking collectives: none -> 100 us  [exchange(): return lax.all_to_all(sent, axes, 0, 0).reshape(count, LANES)]
    psum x3 -> x0, blocking collectives: 66.4 us -> none  [per_device(): grad_own, curv_own = lax.psum((grad_own, curv_own), 'tm')]
    slice x27 -> x0, local copies, waits for them, and re-layouts: 39.5 us -> none  [the longest x15 24.4 us: jones(): array[..., index, :]]
  transfers between devices with their start and end apart: 6 -> 1, of which waited for: 6 -> 1; matrix products, arithmetic and copies ran while one was open for 0% -> 0% of each run, Pallas kernels for 0% -> 0%
where the time goes in v1:
time: 129 us; the launch traced here: 128 us
  blocking collectives  100 us (78%)
  waiting for transfers between devices  9.25 us (7%)
  starting transfers between devices  9.19 us (7%)
  Pallas kernels  6.73 us (5%)
  local copies, waits for them, and re-layouts  1.68 us (1%)
    all_to_all x8, blocking collectives, exchange(): return lax.all_to_all(sent, axes, 0, 0).reshape(count, LANES)  100 us
    all_to_all x1, waiting for transfers between devices, exchange(): return lax.all_to_all(sent, axes, 0, 0).reshape(count, LANES)  9.25 us
    all_to_all x1, starting transfers between devices, exchange(): return lax.all_to_all(sent, axes, 0, 0).reshape(count, LANES)  9.19 us
    pallas_call x3, Pallas kernels, partials(): pl.pallas_call(partials_kernel, out_shape=jax.ShapeDtypeStruct((pairs //...  2.79 us
  transfers between devices with their start and end apart: 1, of which 1 were waited for; matrix products, arithmetic and copies ran while one was open for 0% of the time, Pallas kernels for 0%

profile of v1, /device:TPU:1, one launch (start us, length us, event | category | flops | bytes accessed | tf_op | source)
XLA Modules:
  0.0 128.1 jit_solution(6090199128223417883)
XLA Ops:
  0.6 0.8 copy.10
  1.4 0.1 broadcast_in_dim.7
  1.5 0.1 broadcast_in_dim.8
  1.6 0.0 copy-start
  1.6 0.0 copy-start.1
  1.6 20.0 %all_to_all.45 = f32[32,1,1024]{2,1,0:T(1,128)S(1)} all-to-all(f32[32,1,1024]{2,1,0:T(1,128)S(1)} %broadcast_in_dim.8), channel_id=1, replica_groups=mesh['y'=8,'x'=4,'z'=4,'core'=2,'chan'=2] {'x','z','core'}, dimensions={0} | all-to-all | bytes 262144 | tf_op jit(solution)/shard_map/all_to_all | solution.py:262
  21.7 0.0 copy-start.4
  21.7 0.0 copy-start.5
  21.7 0.0 copy-start.2
  21.7 0.0 copy-start.3
  21.7 0.0 copy-done
  21.7 0.0 copy-done.1
  21.7 0.6 copy-done.4
  22.3 0.0 copy-done.5
  22.4 0.0 copy-done.2
  22.4 0.0 copy-done.3
  22.4 0.9 partials.3
  23.3 10.1 %all_to_all.46 = f32[16,1,2304]{2,1,0:T(1,128)S(1)} all-to-all(f32[16,1,2304]{2,1,0:T(1,128)S(1)} %bitcast.43), channel_id=1, replica_groups=mesh['y'=8,'x'=4,'z'=4,'core'=2,'chan'=2] {'x','z'}, dimensions={0} | all-to-all | bytes 294912 | tf_op jit(solution)/shard_map/all_to_all | solution.py:262
  33.4 0.7 total.3
  34.1 9.2 %all-to-all-start.2 = ((f32[16,1,2304]{2,1,0:T(1,128)}), f32[16,1,2304]{2,1,0:T(1,128)S(1)}, u32[]{:S(2)}, u32[]{:S(2)}) async-start(f32[16,1,2304]{2,1,0:T(1,128)} %bitcast.13), calls=%async_computation.2 | async-start | bytes 294912 | tf_op jit(solution)/shard_map/all_to_all | solution.py:262
  43.3 0.1 pad_add_fusion.at_ref
  43.3 9.2 %all-to-all-done.2 = f32[16,1,2304]{2,1,0:T(1,128)S(1)} async-done(((f32[16,1,2304]{2,1,0:T(1,128)}), f32[16,1,2304]{2,1,0:T(1,128)S(1)}, u32[]{:S(2)}, u32[]{:S(2)}) %all-to-all-start.2) | async-done | bytes 147488 | tf_op jit(solution)/shard_map/all_to_all | solution.py:262
  52.6 0.7 step.2
  53.3 10.0 %all_to_all.47 = f32[16,1,2048]{2,1,0:T(1,128)S(1)} all-to-all(f32[16,1,2048]{2,1,0:T(1,128)S(1)} %bitcast.49), channel_id=1, replica_groups=mesh['y'=8,'x'=4,'z'=4,'core'=2,'chan'=2] {'x','z'}, dimensions={0} | all-to-all | bytes 262144 | tf_op jit(solution)/shard_map/all_to_all | solution.py:262
  63.3 0.9 partials.4
  64.3 11.2 %all_to_all.48 = f32[16,1,2304]{2,1,0:T(1,128)S(1)} all-to-all(f32[16,1,2304]{2,1,0:T(1,128)S(1)} %bitcast.44), channel_id=1, replica_groups=mesh['y'=8,'x'=4,'z'=4,'core'=2,'chan'=2] {'x','z'}, dimensions={0} | all-to-all | bytes 294912 | tf_op jit(solution)/shard_map/all_to_all | solution.py:262
  75.5 14.0 %all_to_all.49 = f32[16,1,2304]{2,1,0:T(1,128)S(1)} all-to-all(f32[16,1,2304]{2,1,0:T(1,128)S(1)} %bitcast.40), channel_id=1, replica_groups=mesh['y'=8,'x'=4,'z'=4,'core'=2,'chan'=2] {'y','core'}, dimensions={0} | all-to-all | bytes 294912 | tf_op jit(solution)/shard_map/all_to_all | solution.py:262
  89.4 0.7 step.3
  90.2 10.5 %all_to_all.50 = f32[16,1,2048]{2,1,0:T(1,128)S(1)} all-to-all(f32[16,1,2048]{2,1,0:T(1,128)S(1)} %bitcast.50), channel_id=1, replica_groups=mesh['y'=8,'x'=4,'z'=4,'core'=2,'chan'=2] {'x','z'}, dimensions={0} | all-to-all | bytes 262144 | tf_op jit(solution)/shard_map/all_to_all | solution.py:262
  100.7 0.9 partials.5
  101.6 10.7 %all_to_all.51 = f32[16,1,2304]{2,1,0:T(1,128)S(1)} all-to-all(f32[16,1,2304]{2,1,0:T(1,128)S(1)} %bitcast.45), channel_id=1, replica_groups=mesh['y'=8,'x'=4,'z'=4,'core'=2,'chan'=2] {'x','z'}, dimensions={0} | all-to-all | bytes 294912 | tf_op jit(solution)/shard_map/all_to_all | solution.py:262
  112.4 14.0 %all_to_all.52 = f32[16,1,2304]{2,1,0:T(1,128)S(1)} all-to-all(f32[16,1,2304]{2,1,0:T(1,128)S(1)} %bitcast.42), channel_id=1, replica_groups=mesh['y'=8,'x'=4,'z'=4,'core'=2,'chan'=2] {'y','core'}, dimensions={0} | all-to-all | bytes 294912 | tf_op jit(solution)/shard_map/all_to_all | solution.py:262
  126.3 1.7 %last.1 = (f32[64,16]{1,0:T(8,128)}, f32[64,16]{1,0:T(8,128)}) custom-call(s32[2]{0:T(128)S(1)} %pad_add_fusion.at_ref, f32[288,128]{1,0:T(8,128)S(1)} %bitcast.36, f32[256,128]{1,0:T(8,128)S(1)} %bitcast.32), custom_call_target="tpu_custom_call" | custom-call | tf_op jit(solution)/shard_map/last/pallas_call | solution.py:247
  (2 shorter events, 0.1 us)
Async XLA Ops:
  1.6 20.1 %copy-start = (bf16[1,2,8,8,256]{4,3,2,1,0:T(8,128)(2,1)S(1)}, bf16[1,2,8,8,256]{4,3,2,1,0:T(8,128)(2,1)}, u32[]{:S(2)}) copy-start(bf16[1,2,8,8,256]{4,3,2,1,0:T(8,128)(2,1)} %param.7) | copy-start | bytes 196612
  1.6 20.1 %copy-start.1 = (f32[1,2,8,256]{3,2,1,0:T(8,128)S(1)}, f32[1,2,8,256]{3,2,1,0:T(8,128)}, u32[]{:S(2)}) copy-start(f32[1,2,8,256]{3,2,1,0:T(8,128)} %param.8) | copy-start | bytes 49156
  21.7 0.7 copy-start.4
  21.7 0.7 copy-start.5
  21.7 0.7 copy-start.2
  21.7 0.7 copy-start.3
  34.1 18.5 %all-to-all-start.2 = ((f32[16,1,2304]{2,1,0:T(1,128)}), f32[16,1,2304]{2,1,0:T(1,128)S(1)}, u32[]{:S(2)}, u32[]{:S(2)}) async-start(f32[16,1,2304]{2,1,0:T(1,128)} %bitcast.13), calls=%async_computation.2 | async-start | bytes 294912 | tf_op jit(solution)/shard_map/all_to_all | solution.py:262

commit v2 on v1

--- a/solution.py
+++ b/solution.py
@@ -69,6 +69,11 @@
     return total
 
 
+def placed(station):
+    kept = station & 0b110001111
+    return kept | ((station & 0b110000) << 1) | ((station >> 2) & 0b10000)
+
+
 def partials_kernel(
     gains_ref, model_ref, vis_ref, weight_ref, live_ref, first_ref, second_ref,
     out_ref, picked_ref, model_f_ref, terms_ref,
@@ -76,7 +81,7 @@
     base = first_ref.shape[1]
     pairs = gains_ref.shape[0]
     channels = model_ref.shape[0]
-    station = jnp.concatenate([first_ref[...], second_ref[...]], axis=1)
+    station = placed(jnp.concatenate([first_ref[...], second_ref[...]], axis=1))
     rows = lax.broadcasted_iota(jnp.int32, (pairs, 2 * base), 0)
     hot = jnp.where(rows == station // 2, 1.0, 0.0).astype(jnp.bfloat16)
     odd = station % 2 == 1
@@ -266,27 +271,27 @@
     base = antenna1.shape[0]
     channels = model.shape[1]
     owned = gains.shape[3]
-    chips, others = ("x", "z"), ("y", "core")
+    near, far = ("x", "z0", "core"), ("y", "z1")
     model = model.reshape(channels, VALS, base)
     vis, weights = vis[0], weights[0]
     first, second, live = (a.reshape(1, base) for a in (antenna1, antenna2, live))
     mine = gains.reshape(VALS, owned).T.reshape(1, owned * VALS // LANES, LANES)
     mine = jnp.broadcast_to(mine, (32,) + mine.shape[1:]).reshape(-1, LANES)
-    full = exchange(mine, ("x", "z", "core"), 32)
-    chip = lax.axis_index("x") * 4 + lax.axis_index("z")
-    at = jnp.stack([chip * RUN, lax.axis_index("core") * (RUN // 2)]).astype(jnp.int32)
+    full = exchange(mine, near + ("z1",), 32)
+    place = lax.axis_index(near)
+    at = jnp.stack([place * RUN, lax.axis_index("z1") * (RUN // 2)]).astype(jnp.int32)
     for turn in range(ITERS):
         sent = partials(full, model, vis, weights, live, first, second)
-        sent = total(exchange(sent, chips, 16), 16)
-        sums = exchange(sent, others, 16)
+        sent = total(exchange(sent, near, 16), 16)
+        sums = exchange(sent, far, 16)
         if turn < ITERS - 1:
-            full = exchange(step(at, sums, full, 16), chips, 16)
+            full = exchange(step(at, sums, full, 16), near, 16)
     return tuple(out.reshape(gains.shape) for out in last(at, sums, full))
 
 
 def solution(mesh):
-    fine = Mesh(mesh.devices.reshape(8, 4, 4, 2, 2), ("y", "x", "z", "core", "chan"))
-    bl = ("x", "z", "core")
+    fine = Mesh(mesh.devices.reshape(8, 4, 2, 2, 2, 2), ("y", "x", "z1", "z0", "core", "chan"))
+    bl = ("x", "z1", "z0", "core")
     return jax.shard_map(
         per_device,
         mesh=fine,

time: 129 us -> 121 us (0.938)
  blocking collectives: 100 us -> 94.4 us
  starting transfers between devices: 9.19 us -> 7.14 us
    all_to_all x8, blocking collectives: 100 us -> 94.4 us  [exchange(): return lax.all_to_all(sent, axes, 0, 0).reshape(count, LANES)]
    all_to_all x1, starting transfers between devices: 9.19 us -> 7.14 us  [exchange(): return lax.all_to_all(sent, axes, 0, 0).reshape(count, LANES)]
where the time goes in v2:
time: 121 us; the launch traced here: 120 us
  blocking collectives  94.4 us (78%)
  waiting for transfers between devices  9.42 us (8%)
  starting transfers between devices  7.14 us (6%)
  Pallas kernels  6.74 us (6%)
  local copies, waits for them, and re-layouts  1.68 us (1%)
    all_to_all x8, blocking collectives, exchange(): return lax.all_to_all(sent, axes, 0, 0).reshape(count, LANES)  94.4 us
    all_to_all x1, waiting for transfers between devices, exchange(): return lax.all_to_all(sent, axes, 0, 0).reshape(count, LANES)  9.42 us
    all_to_all x1, starting transfers between devices, exchange(): return lax.all_to_all(sent, axes, 0, 0).reshape(count, LANES)  7.14 us
    pallas_call x3, Pallas kernels, partials(): pl.pallas_call(partials_kernel, out_shape=jax.ShapeDtypeStruct((pairs //...  2.79 us
  transfers between devices with their start and end apart: 1, of which 1 were waited for; matrix products, arithmetic and copies ran while one was open for 0% of the time, Pallas kernels for 0%

profile of v2, /device:TPU:1, one launch (start us, length us, event | category | flops | bytes accessed | tf_op | source)
XLA Modules:
  0.0 120.2 jit_solution(10442834128854185984)
XLA Ops:
  0.6 0.8 copy.10
  1.4 0.1 broadcast_in_dim.7
  1.5 0.1 broadcast_in_dim.8
  1.6 0.0 copy-start
  1.6 0.0 copy-start.1
  1.6 20.0 %all_to_all.45 = f32[32,1,1024]{2,1,0:T(1,128)S(1)} all-to-all(f32[32,1,1024]{2,1,0:T(1,128)S(1)} %broadcast_in_dim.8), channel_id=1, replica_groups=mesh['y'=8,'x'=4,'z1'=2,'z0'=2,'core'=2,'chan'=2] {'x','z0','core','z1'}, dimensions={0} | all-to-all | bytes 262144 | tf_op jit(solution)/shard_map/all_to_all | solution.py:267
  21.6 0.0 copy-start.4
  21.6 0.0 copy-start.5
  21.6 0.0 copy-start.2
  21.6 0.0 copy-start.3
  21.6 0.0 copy-done
  21.6 0.0 copy-done.1
  21.7 0.6 copy-done.4
  22.3 0.0 copy-done.5
  22.3 0.0 copy-done.2
  22.3 0.0 copy-done.3
  22.3 0.9 partials.3
  23.3 9.3 %all_to_all.46 = f32[16,1,2304]{2,1,0:T(1,128)S(1)} all-to-all(f32[16,1,2304]{2,1,0:T(1,128)S(1)} %bitcast.43), channel_id=1, replica_groups=mesh['y'=8,'x'=4,'z1'=2,'z0'=2,'core'=2,'chan'=2] {'x','z0','core'}, dimensions={0} | all-to-all | bytes 294912 | tf_op jit(solution)/shard_map/all_to_all | solution.py:267
  32.6 0.7 total.3
  33.3 7.1 %all-to-all-start.2 = ((f32[16,1,2304]{2,1,0:T(1,128)}), f32[16,1,2304]{2,1,0:T(1,128)S(1)}, u32[]{:S(2)}, u32[]{:S(2)}) async-start(f32[16,1,2304]{2,1,0:T(1,128)} %bitcast.13), calls=%async_computation.2 | async-start | bytes 294912 | tf_op jit(solution)/shard_map/all_to_all | solution.py:267
  40.4 0.1 pad_add_fusion.at_ref
  40.5 9.4 %all-to-all-done.2 = f32[16,1,2304]{2,1,0:T(1,128)S(1)} async-done(((f32[16,1,2304]{2,1,0:T(1,128)}), f32[16,1,2304]{2,1,0:T(1,128)S(1)}, u32[]{:S(2)}, u32[]{:S(2)}) %all-to-all-start.2) | async-done | bytes 147488 | tf_op jit(solution)/shard_map/all_to_all | solution.py:267
  49.9 0.7 step.2
  50.7 10.9 %all_to_all.47 = f32[16,1,2048]{2,1,0:T(1,128)S(1)} all-to-all(f32[16,1,2048]{2,1,0:T(1,128)S(1)} %bitcast.49), channel_id=1, replica_groups=mesh['y'=8,'x'=4,'z1'=2,'z0'=2,'core'=2,'chan'=2] {'x','z0','core'}, dimensions={0} | all-to-all | bytes 262144 | tf_op jit(solution)/shard_map/all_to_all | solution.py:267
  61.6 0.9 partials.4
  62.5 9.4 %all_to_all.48 = f32[16,1,2304]{2,1,0:T(1,128)S(1)} all-to-all(f32[16,1,2304]{2,1,0:T(1,128)S(1)} %bitcast.44), channel_id=1, replica_groups=mesh['y'=8,'x'=4,'z1'=2,'z0'=2,'core'=2,'chan'=2] {'x','z0','core'}, dimensions={0} | all-to-all | bytes 294912 | tf_op jit(solution)/shard_map/all_to_all | solution.py:267
  72.0 12.2 %all_to_all.49 = f32[16,1,2304]{2,1,0:T(1,128)S(1)} all-to-all(f32[16,1,2304]{2,1,0:T(1,128)S(1)} %bitcast.40), channel_id=1, replica_groups=mesh['y'=8,'x'=4,'z1'=2,'z0'=2,'core'=2,'chan'=2] {'y','z1'}, dimensions={0} | all-to-all | bytes 294912 | tf_op jit(solution)/shard_map/all_to_all | solution.py:267
  84.2 0.7 step.3
  84.9 11.0 %all_to_all.50 = f32[16,1,2048]{2,1,0:T(1,128)S(1)} all-to-all(f32[16,1,2048]{2,1,0:T(1,128)S(1)} %bitcast.50), channel_id=1, replica_groups=mesh['y'=8,'x'=4,'z1'=2,'z0'=2,'core'=2,'chan'=2] {'x','z0','core'}, dimensions={0} | all-to-all | bytes 262144 | tf_op jit(solution)/shard_map/all_to_all | solution.py:267
  95.9 0.9 partials.5
  96.8 9.4 %all_to_all.51 = f32[16,1,2304]{2,1,0:T(1,128)S(1)} all-to-all(f32[16,1,2304]{2,1,0:T(1,128)S(1)} %bitcast.45), channel_id=1, replica_groups=mesh['y'=8,'x'=4,'z1'=2,'z0'=2,'core'=2,'chan'=2] {'x','z0','core'}, dimensions={0} | all-to-all | bytes 294912 | tf_op jit(solution)/shard_map/all_to_all | solution.py:267
  106.3 12.2 %all_to_all.52 = f32[16,1,2304]{2,1,0:T(1,128)S(1)} all-to-all(f32[16,1,2304]{2,1,0:T(1,128)S(1)} %bitcast.42), channel_id=1, replica_groups=mesh['y'=8,'x'=4,'z1'=2,'z0'=2,'core'=2,'chan'=2] {'y','z1'}, dimensions={0} | all-to-all | bytes 294912 | tf_op jit(solution)/shard_map/all_to_all | solution.py:267
  118.5 1.7 %last.1 = (f32[64,16]{1,0:T(8,128)}, f32[64,16]{1,0:T(8,128)}) custom-call(s32[2]{0:T(128)S(1)} %pad_add_fusion.at_ref, f32[288,128]{1,0:T(8,128)S(1)} %bitcast.36, f32[256,128]{1,0:T(8,128)S(1)} %bitcast.32), custom_call_target="tpu_custom_call" | custom-call | tf_op jit(solution)/shard_map/last/pallas_call | solution.py:252
  (2 shorter events, 0.1 us)
Async XLA Ops:
  1.6 20.0 %copy-start = (bf16[1,2,8,8,256]{4,3,2,1,0:T(8,128)(2,1)S(1)}, bf16[1,2,8,8,256]{4,3,2,1,0:T(8,128)(2,1)}, u32[]{:S(2)}) copy-start(bf16[1,2,8,8,256]{4,3,2,1,0:T(8,128)(2,1)} %param.7) | copy-start | bytes 196612
  1.6 20.0 %copy-start.1 = (f32[1,2,8,256]{3,2,1,0:T(8,128)S(1)}, f32[1,2,8,256]{3,2,1,0:T(8,128)}, u32[]{:S(2)}) copy-start(f32[1,2,8,256]{3,2,1,0:T(8,128)} %param.8) | copy-start | bytes 49156
  21.6 0.7 copy-start.4
  21.6 0.7 copy-start.5
  21.6 0.7 copy-start.2
  21.6 0.7 copy-start.3
  33.3 16.7 %all-to-all-start.2 = ((f32[16,1,2304]{2,1,0:T(1,128)}), f32[16,1,2304]{2,1,0:T(1,128)S(1)}, u32[]{:S(2)}, u32[]{:S(2)}) async-start(f32[16,1,2304]{2,1,0:T(1,128)} %bitcast.13), calls=%async_computation.2 | async-start | bytes 294912 | tf_op jit(solution)/shard_map/all_to_all | solution.py:267

commit v3 on v2

v3 whole, which is shorter than its diff:
```python
import functools

import jax
import jax.numpy as jnp
from jax import lax
from jax.experimental import pallas as pl
from jax.experimental.pallas import tpu as pltpu
from jax.sharding import Mesh
from jax.sharding import PartitionSpec as P

ITERS = 3
STEP = 0.8
DIRS = 8
COMPS = 8
VALS = DIRS * COMPS
LANES = 128
RUN = LANES // DIRS


def cmul(left, right):
    return (left[0] * right[0] - left[1] * right[1], left[0] * right[1] + left[1] * right[0])


def cadd(left, right):
    return (left[0] + right[0], left[1] + right[1])


def adjoint(matrix):
    return [(entry[0], -entry[1]) for entry in (matrix[0], matrix[2], matrix[1], matrix[3])]


def product(left, right):
    result = []
    for row in range(2):
        for col in range(2):
            result.append(
                cadd(cmul(left[2 * row], right[col]), cmul(left[2 * row + 1], right[2 + col]))
            )
    return result


def norm_sq(matrix):
    return sum(entry[0] * entry[0] + entry[1] * entry[1] for entry in matrix)


def halves(value):
    high = value.astype(jnp.bfloat16)
    low = (value - high.astype(jnp.float32)).astype(jnp.bfloat16)
    return high, low


def select_sum(left, right, dims):
    total = None
    for part in halves(left):
        term = lax.dot_general(
            part, right, (dims, ((), ())), preferred_element_type=jnp.float32
        )
        total = term if total is None else total + term
    return total


def pick_sum(left, right, dims):
    total = None
    for part in halves(right):
        term = lax.dot_general(
            left, part, (dims, ((), ())), preferred_element_type=jnp.float32
        )
        total = term if total is None else total + term
    return total


def placed(station):
    kept = station & 0b110001111
    return kept | ((station & 0b110000) << 1) | ((station >> 2) & 0b10000)


def in_vmem(count):
    return [pl.BlockSpec(memory_space=pltpu.VMEM)] * count


PARAMS = pltpu.CompilerParams(vmem_limit_bytes=16 * 2**20)


def pack_kernel(model_ref, vis_ref, weight_ref, live_ref, gains_ref, data_ref, copies_ref):
    channels, base = weight_ref.shape
    cuts = base // LANES
    live = live_ref[...].astype(jnp.float32)
    scales = []
    for part in range(channels * cuts):
        channel, cut = divmod(part, cuts)
        lanes = slice(cut * LANES, (cut + 1) * LANES)
        at = part * (VALS + COMPS)
        data_ref[at : at + VALS, :] = model_ref[channel, :, lanes].astype(jnp.float32)
        data_ref[at + VALS : at + VALS + COMPS, :] = vis_ref[channel, :, lanes]
        scales.append(weight_ref[channel : channel + 1, lanes] * live[:, lanes])
    at = len(scales) * (VALS + COMPS)
    spare = data_ref.shape[0] - at - len(scales)
    scales.append(jnp.zeros((spare, LANES), jnp.float32))
    data_ref[at:, :] = jnp.concatenate(scales, axis=0)

    owned = gains_ref.shape[1]
    target = lax.broadcasted_iota(jnp.int32, (owned // 2, owned), 0)
    source = lax.broadcasted_iota(jnp.int32, (owned // 2, owned), 1)
    mine = jnp.concatenate(
        [
            lax.dot_general(
                jnp.where(source == 2 * target + odd, 1.0, 0.0),
                gains_ref[...],
                (((1,), (1,)), ((), ())),
                precision=lax.Precision.HIGHEST,
                preferred_element_type=jnp.float32,
            )
            for odd in range(2)
        ],
        axis=1,
    )
    for at in range(0, copies_ref.shape[0], owned // 2):
        copies_ref[at : at + owned // 2, :] = mine


def pack(model, vis, weights, live, gains, peers):
    channels, base = weights.shape
    parts = channels * base // LANES
    rows = parts * (VALS + COMPS) + -(-parts // 8) * 8
    owned = gains.shape[1]
    return pl.pallas_call(
        pack_kernel,
        out_shape=(
            jax.ShapeDtypeStruct((rows, LANES), jnp.float32),
            jax.ShapeDtypeStruct((peers * owned // 2, LANES), jnp.float32),
        ),
        in_specs=in_vmem(5),
        out_specs=tuple(in_vmem(2)),
        compiler_params=PARAMS,
        name="pack",
    )(model, vis, weights, live, gains)


def partials_kernel(
    run, channels, gains_ref, data_ref, first_ref, second_ref, out_ref, picked_ref, terms_ref
):
    base = first_ref.shape[1]
    pairs = gains_ref.shape[0]
    times = data_ref.shape[0]
    cuts = base // LANES
    station = placed(jnp.concatenate([first_ref[...], second_ref[...]], axis=1))
    rows = lax.broadcasted_iota(jnp.int32, (pairs, 2 * base), 0)
    hot = jnp.where(rows == station // 2, 1.0, 0.0).astype(jnp.bfloat16)
    odd = station % 2 == 1

    both = select_sum(gains_ref[...].T, hot, ((1,), (0,)))
    picked = jnp.where(odd, both[VALS:], both[:VALS])
    for cut in range(2 * cuts):
        picked_ref[cut] = picked[:, cut * LANES : (cut + 1) * LANES]

    def entries(ref, outer, at):
        comps = [ref[outer, pl.ds(at + c, DIRS, stride=COMPS), :] for c in range(COMPS)]
        return [(comps[i], comps[i + 4]) for i in range(4)]

    curvs = [None] * (2 * cuts)
    for cut in range(cuts):
        near = entries(picked_ref, cut, 0)
        far = entries(picked_ref, cuts + cut, 0)

        def at_time(time, totals, cut=cut, near=near, far=far):
            for channel in range(channels):
                part = channel * cuts + cut
                at = part * (VALS + COMPS)
                model = entries(data_ref, time, at)
                vis = data_ref[time, at + VALS : at + VALS + COMPS, :]
                row = channels * cuts * (VALS + COMPS) + part
                scale = data_ref[time, row : row + 1, :]
                right_a = product(model, adjoint(far))
                left_b = product(near, model)
                each = product(near, right_a)
                resid = []
                for index in range(4):
                    pred_re = jnp.sum(each[index][0], axis=0, keepdims=True)
                    pred_im = jnp.sum(each[index][1], axis=0, keepdims=True)
                    resid.append(
                        (
                            scale * (vis[index : index + 1] - pred_re),
                            scale * (vis[index + 4 : index + 5] - pred_im),
                        )
                    )
                new = (
                    product(resid, adjoint(right_a)),
                    product(adjoint(resid), left_b),
                    scale * norm_sq(right_a),
                    scale * norm_sq(left_b),
                )
                totals = new if totals is None else jax.tree.map(jnp.add, totals, new)
            return totals

        totals = at_time(0, None)
        if times > 1:
            totals = lax.fori_loop(1, times, at_time, totals)
        for side in range(2):
            at = side * cuts + cut
            for index, (real, imag) in enumerate(totals[side]):
                terms_ref[at, pl.ds(index, DIRS, stride=COMPS), :] = -real
                terms_ref[at, pl.ds(index + 4, DIRS, stride=COMPS), :] = -imag
            curvs[at] = totals[2 + side]

    terms = jnp.concatenate([terms_ref[at] for at in range(2 * cuts)], axis=1)
    curv = jnp.concatenate(curvs, axis=1)
    spread = jnp.concatenate([jnp.where(odd, 0.0, terms), jnp.where(odd, terms, 0.0)], axis=0)
    grads = pick_sum(hot, spread, ((1,), (1,)))
    place = station % RUN
    spread = jnp.concatenate([jnp.where(place == j, curv, 0.0) for j in range(RUN)], axis=0)
    rows = lax.broadcasted_iota(jnp.int32, (2 * pairs // RUN, 2 * base), 0)
    hot = jnp.where(rows == station // RUN, 1.0, 0.0).astype(jnp.bfloat16)
    curvs = pick_sum(hot, spread, ((1,), (1,)))
    extra = run // 8
    for peer in range(pairs // run):
        at = peer * (run + extra)
        out_ref[at : at + run, :] = grads[peer * run : (peer + 1) * run]
        out_ref[at + run : at + run + extra, :] = curvs[peer * extra : (peer + 1) * extra]


def partials(run, channels, gains, data, first, second):
    pairs = gains.shape[0]
    base = first.shape[1]
    return pl.pallas_call(
        functools.partial(partials_kernel, run, channels),
        out_shape=jax.ShapeDtypeStruct((pairs // 8 * 9, LANES), jnp.float32),
        in_specs=in_vmem(4),
        out_specs=in_vmem(1)[0],
        scratch_shapes=[pltpu.VMEM((2 * base // LANES, VALS, LANES), jnp.float32)] * 2,
        compiler_params=PARAMS,
        name="partials",
    )(gains, data, first, second)


def peers_sum(parts_ref, rows):
    total = parts_ref[0:rows, :]
    for at in range(rows, parts_ref.shape[0], rows):
        total = total + parts_ref[at : at + rows, :]
    return total


def total_kernel(rows, parts_ref, copies_ref):
    total = peers_sum(parts_ref, rows)
    for at in range(0, copies_ref.shape[0], rows):
        copies_ref[at : at + rows, :] = total


def total(run, parts, peers):
    rows = run // 8 * 9
    return pl.pallas_call(
        functools.partial(total_kernel, rows),
        out_shape=jax.ShapeDtypeStruct((peers * rows, LANES), jnp.float32),
        in_specs=in_vmem(1),
        out_specs=in_vmem(1)[0],
        compiler_params=PARAMS,
        name="total",
    )(parts)


def stepped(run, at_ref, parts_ref, gains_ref):
    sums = peers_sum(parts_ref, run // 8 * 9)
    grad = sums[:run]
    row = lax.broadcasted_iota(jnp.int32, (run, LANES), 0)
    lane = lax.broadcasted_iota(jnp.int32, (run, LANES), 1)
    curv = sums[run : run + 1]
    for extra in range(1, run // 8):
        curv = jnp.where(row < 8 * extra, curv, sums[run + extra : run + extra + 1])
    curv = jnp.where(lane // (2 * DIRS) == row % 8, curv, 0.0)
    source = lax.broadcasted_iota(jnp.int32, (LANES, LANES), 0)
    target = lax.broadcasted_iota(jnp.int32, (LANES, LANES), 1)
    wide = jnp.where(source % (2 * DIRS) == target // COMPS, 1.0, 0.0)
    denom = 1.0 + jnp.dot(
        curv, wide, precision=lax.Precision.HIGHEST, preferred_element_type=jnp.float32
    )
    old = gains_ref[pl.ds(pl.multiple_of(at_ref[0], run), run), :]
    return old - STEP * grad / denom, grad / jnp.sqrt(denom)


def step_kernel(run, at_ref, parts_ref, gains_ref, copies_ref):
    gains, _ = stepped(run, at_ref, parts_ref, gains_ref)
    for at in range(0, copies_ref.shape[0], run):
        copies_ref[at : at + run, :] = gains


def last_kernel(run, at_ref, parts_ref, gains_ref, gains_out_ref, white_ref):
    owned = 2 * run
    source = lax.broadcasted_iota(jnp.int32, (run, owned), 0)
    target = lax.broadcasted_iota(jnp.int32, (run, owned), 1)
    results = stepped(run, at_ref, parts_ref, gains_ref)
    for value, out_ref in zip(results, (gains_out_ref, white_ref)):
        turned = value.T
        out = None
        for odd in range(2):
            place = jnp.where(target == 2 * source + odd, 1.0, 0.0)
            part = jnp.dot(
                turned[odd * VALS : (odd + 1) * VALS],
                place,
                precision=lax.Precision.HIGHEST,
                preferred_element_type=jnp.float32,
            )
            out = part if out is None else out + part
        out_ref[...] = out


def step(run, at, parts, gains):
    return pl.pallas_call(
        functools.partial(step_kernel, run),
        out_shape=jax.ShapeDtypeStruct(gains.shape, jnp.float32),
        in_specs=[pl.BlockSpec(memory_space=pltpu.SMEM)] + in_vmem(2),
        out_specs=in_vmem(1)[0],
        compiler_params=PARAMS,
        name="step",
    )(at, parts, gains)


def last(run, at, parts, gains):
    return pl.pallas_call(
        functools.partial(last_kernel, run),
        out_shape=(jax.ShapeDtypeStruct((VALS, 2 * run), jnp.float32),) * 2,
        in_specs=[pl.BlockSpec(memory_space=pltpu.SMEM)] + in_vmem(2),
        out_specs=tuple(in_vmem(2)),
        compiler_params=PARAMS,
        name="last",
    )(at, parts, gains)


def exchange(rows, axes, peers):
    count = rows.shape[0]
    sent = rows.reshape(peers, 1, count // peers * LANES)
    return lax.all_to_all(sent, axes, 0, 0).reshape(count, LANES)


def per_device(model, vis, weights, antenna1, antenna2, live, gains):
    base = antenna1.shape[0]
    channels = model.shape[1]
    near, far = ("x", "z0", "core"), ("y", "z1")
    wide = near + ("z1",)
    first, second, live = (a.reshape(1, base) for a in (antenna1, antenna2, live))
    data, copies = pack(
        model.reshape(channels, VALS, base), vis[0], weights[0], live,
        gains.reshape(VALS, gains.shape[3]), 32,
    )
    every = lax.all_gather(data, "y")
    full = exchange(copies, wide, 32)

    at = (lax.axis_index(near) * 16).reshape(1).astype(jnp.int32)
    sent = partials(16, channels, full, data[None], first, second)
    sent = total(16, exchange(sent, near, 16), 16)
    full = exchange(step(16, at, exchange(sent, far, 16), full), near, 16)

    at = (lax.axis_index(wide) * 8).reshape(1).astype(jnp.int32)
    for turn in range(1, ITERS):
        sums = exchange(partials(8, channels, full, every, first, second), wide, 32)
        if turn < ITERS - 1:
            full = exchange(step(8, at, sums, full), wide, 32)
    return tuple(out.reshape(gains.shape) for out in last(8, at, sums, full))


def solution(mesh):
    fine = Mesh(mesh.devices.reshape(8, 4, 2, 2, 2, 2), ("y", "x", "z1", "z0", "core", "chan"))
    bl = ("x", "z1", "z0", "core")
    return jax.shard_map(
        per_device,
        mesh=fine,
        in_specs=(
            P("y", "chan", None, None, bl),
            P("y", "chan", None, bl),
            P("y", "chan", bl),
            P(bl),
            P(bl),
            P(bl),
            P("chan", None, None, bl),
        ),
        out_specs=(P("chan", None, None, bl), P("chan", None, None, bl)),
        check_vma=False,
    )
```

time: 121 us -> 127 us (1.050)
  blocking collectives: 94.4 us -> 65.2 us
  between operations: 0.73 us -> 14.1 us
  waiting for transfers between devices: 9.42 us -> 18.6 us
  local copies, waits for them, and re-layouts: 1.68 us -> 6.31 us
  starting transfers between devices: 7.14 us -> 11.3 us
  Pallas kernels: 6.74 us -> 10.9 us
    all_to_all x8 -> x5, blocking collectives: 94.4 us -> 65.2 us  [exchange(): return lax.all_to_all(sent, axes, 0, 0).reshape(count, LANES)]
    all_to_all x1 -> x2, waiting for transfers between devices: 9.42 us -> 18.6 us  [exchange(): return lax.all_to_all(sent, axes, 0, 0).reshape(count, LANES)]
    unnamed x12 -> x22, local copies, waits for them, and re-layouts: 0.71 us -> 6.31 us
    all_to_all x1 -> x2, starting transfers between devices: 7.14 us -> 11.3 us  [exchange(): return lax.all_to_all(sent, axes, 0, 0).reshape(count, LANES)]
    pallas_call x9 -> x8, Pallas kernels: 6.74 us -> 10.9 us  [the longest x3 7.81 us: partials(): pl.pallas_call(functools.partial(partials_kernel, run, channels), out_sha...]
  transfers between devices with their start and end apart: 1 -> 3, of which waited for: 1 -> 2; matrix products, arithmetic and copies ran while one was open for 0% -> 0% of each run, Pallas kernels for 0% -> 2%
where the time goes in v3:
time: 127 us; the launch traced here: 126 us
  blocking collectives  65.2 us (51%)
  waiting for transfers between devices  18.6 us (15%)
  between operations  14.1 us (11%)
  starting transfers between devices  11.3 us (9%)
  Pallas kernels  10.9 us (9%)
  local copies, waits for them, and re-layouts  6.31 us (5%)
    all_to_all x5, blocking collectives, exchange(): return lax.all_to_all(sent, axes, 0, 0).reshape(count, LANES)  65.2 us
    all_to_all x2, waiting for transfers between devices, exchange(): return lax.all_to_all(sent, axes, 0, 0).reshape(count, LANES)  18.6 us
    all_to_all x2, starting transfers between devices, exchange(): return lax.all_to_all(sent, axes, 0, 0).reshape(count, LANES)  11.3 us
    pallas_call x3, Pallas kernels, partials(): pl.pallas_call(functools.partial(partials_kernel, run, channels), out_sha...  7.81 us
    unnamed x22, local copies, waits for them, and re-layouts  6.31 us
  transfers between devices with their start and end apart: 3, of which 2 were waited for; matrix products, arithmetic and copies ran while one was open for 0% of the time, Pallas kernels for 2%

profile of v3, /device:TPU:1, one launch (start us, length us, event | category | flops | bytes accessed | tf_op | source)
XLA Modules:
  0.0 126.5 jit_solution(11685430460830740343)
XLA Ops:
  7.2 0.0 all-gather.3.cloned.1.call-start
  7.2 0.0 copy-start.2
  7.2 0.8 copy-done.2
  8.1 0.0 copy-start.3
  8.1 0.8 copy-done.3
  8.8 0.0 copy-start.4
  8.8 0.7 copy-done.4
  9.5 0.0 copy-start.9
  9.5 0.7 copy-done.9
  10.2 0.0 copy-start.10
  10.2 0.7 copy-done.10
  10.9 0.8 pack.1
  11.6 0.0 copy-start.6
  11.7 0.0 copy-start.8
  11.7 0.0 all-gather.3.cloned.1.call-update
  11.7 19.9 %all_to_all.35 = f32[32,1,1024]{2,1,0:T(1,128)S(1)} all-to-all(f32[32,1,1024]{2,1,0:T(1,128)S(1)} %bitcast.43), channel_id=1, replica_groups=mesh['y'=8,'x'=4,'z1'=2,'z0'=2,'core'=2,'chan'=2] {'x','z0','core','z1'}, dimensions={0} | all-to-all | bytes 262144 | tf_op jit(solution)/shard_map/all_to_all | solution.py:330
  31.5 0.0 copy-start.5
  31.5 0.7 copy-done.5
  32.2 0.0 copy-start.7
  32.2 0.7 copy-done.7
  32.9 1.8 %partials.3 = f32[288,128]{1,0:T(8,128)S(1)} custom-call(f32[256,128]{1,0:T(8,128)S(1)} %bitcast.33, f32[1,296,128]{2,1,0:T(8,128)} %bitcast.9.data_ref, s32[1,256]{1,0:T(1,128)S(1)} %bitcast.47, s32[1,256]{1,0:T(1,128)S(1)} %bitcast.50), custom_call_target="tpu_custom_call" | custom-call | tf_op jit(solution)/shard_map/partials/pallas_call | solution.py:224
  34.7 9.3 %all_to_all.36 = f32[16,1,2304]{2,1,0:T(1,128)S(1)} all-to-all(f32[16,1,2304]{2,1,0:T(1,128)S(1)} %bitcast.40), channel_id=1, replica_groups=mesh['y'=8,'x'=4,'z1'=2,'z0'=2,'core'=2,'chan'=2] {'x','z0','core'}, dimensions={0} | all-to-all | bytes 294912 | tf_op jit(solution)/shard_map/all_to_all | solution.py:330
  44.0 0.7 total.1
  44.7 7.1 %all-to-all-start.2 = ((f32[16,1,2304]{2,1,0:T(1,128)}), f32[16,1,2304]{2,1,0:T(1,128)S(1)}, u32[]{:S(2)}, u32[]{:S(2)}) async-start(f32[16,1,2304]{2,1,0:T(1,128)} %bitcast.14), calls=%async_computation.2 | async-start | bytes 294912 | tf_op jit(solution)/shard_map/all_to_all | solution.py:330
  51.9 9.5 %all-to-all-done.2 = f32[16,1,2304]{2,1,0:T(1,128)S(1)} async-done(((f32[16,1,2304]{2,1,0:T(1,128)}), f32[16,1,2304]{2,1,0:T(1,128)S(1)}, u32[]{:S(2)}, u32[]{:S(2)}) %all-to-all-start.2) | async-done | bytes 147488 | tf_op jit(solution)/shard_map/all_to_all | solution.py:330
  61.4 0.2 step.2
  61.6 11.7 %all_to_all.37 = f32[16,1,2048]{2,1,0:T(1,128)S(1)} all-to-all(f32[16,1,2048]{2,1,0:T(1,128)S(1)} %bitcast.41), channel_id=1, replica_groups=mesh['y'=8,'x'=4,'z1'=2,'z0'=2,'core'=2,'chan'=2] {'x','z0','core'}, dimensions={0} | all-to-all | bytes 262144 | tf_op jit(solution)/shard_map/all_to_all | solution.py:330
  73.4 0.0 all-gather.3.cloned.1.call-done
  73.4 0.0 copy-done.6
  73.4 0.0 copy-done.8
  73.4 0.0 copy-start
  73.4 1.3 %copy-done = f32[2368,128]{1,0:T(8,128)S(1)} copy-done((f32[2368,128]{1,0:T(8,128)S(1)}, f32[2368,128]{1,0:T(8,128)}, u32[]{:S(2)}) %copy-start) | copy-done | bytes 1212440
  74.7 0.0 copy-start.1
  74.7 3.3 %partials.4 = f32[288,128]{1,0:T(8,128)} custom-call(f32[256,128]{1,0:T(8,128)S(1)} %bitcast.29, f32[8,296,128]{2,1,0:T(8,128)S(1)} %bitcast.27, s32[1,256]{1,0:T(1,128)S(1)} %bitcast.48, s32[1,256]{1,0:T(1,128)S(1)} %bitcast.51), custom_call_target="tpu_custom_call" | custom-call | tf_op jit(solution)/shard_map/partials/pallas_call | solution.py:224
  78.0 4.2 %all-to-all-start.4 = ((f32[32,1,1152]{2,1,0:T(1,128)}), f32[32,1,1152]{2,1,0:T(1,128)S(1)}, u32[]{:S(2)}, u32[]{:S(2)}) async-start(f32[32,1,1152]{2,1,0:T(1,128)} %bitcast.19), calls=%async_computation.4 | async-start | bytes 294912 | tf_op jit(solution)/shard_map/all_to_all | solution.py:330
  82.2 9.0 %all-to-all-done.4 = f32[32,1,1152]{2,1,0:T(1,128)S(1)} async-done(((f32[32,1,1152]{2,1,0:T(1,128)}), f32[32,1,1152]{2,1,0:T(1,128)S(1)}, u32[]{:S(2)}, u32[]{:S(2)}) %all-to-all-start.4) | async-done | bytes 147488 | tf_op jit(solution)/shard_map/all_to_all | solution.py:330
  91.2 0.2 step.3
  91.4 12.1 %all_to_all.38 = f32[32,1,1024]{2,1,0:T(1,128)S(1)} all-to-all(f32[32,1,1024]{2,1,0:T(1,128)S(1)} %bitcast.42), channel_id=1, replica_groups=mesh['y'=8,'x'=4,'z1'=2,'z0'=2,'core'=2,'chan'=2] {'x','z0','core','z1'}, dimensions={0} | all-to-all | bytes 262144 | tf_op jit(solution)/shard_map/all_to_all | solution.py:330
  103.5 0.0 copy-done.1
  103.5 2.7 %partials.5 = f32[288,128]{1,0:T(8,128)S(1)} custom-call(f32[256,128]{1,0:T(8,128)S(1)} %bitcast.31, f32[8,296,128]{2,1,0:T(8,128)S(1)} %bitcast.28, s32[1,256]{1,0:T(1,128)S(1)} %bitcast.49, s32[1,256]{1,0:T(1,128)S(1)} %bitcast.52), custom_call_target="tpu_custom_call" | custom-call | tf_op jit(solution)/shard_map/partials/pallas_call | solution.py:224
  106.1 12.3 %all_to_all.39 = f32[32,1,1152]{2,1,0:T(1,128)S(1)} all-to-all(f32[32,1,1152]{2,1,0:T(1,128)S(1)} %bitcast.35), channel_id=1, replica_groups=mesh['y'=8,'x'=4,'z1'=2,'z0'=2,'core'=2,'chan'=2] {'x','z0','core','z1'}, dimensions={0} | all-to-all | bytes 294912 | tf_op jit(solution)/shard_map/all_to_all | solution.py:330
  118.4 1.2 last.1
Async XLA Ops:
  7.2 66.2 %all-gather.3.cloned.1.call-start = ((), (), s32[]{:S(2)}) async-start(), calls=%async_computation.7 | async-start | bytes 1363968 | tf_op jit(solution)/shard_map/all_gather | solution.py:343
  7.2 0.8 copy-start.2
  8.1 0.8 copy-start.3
  8.8 0.7 copy-start.4
  9.5 0.7 copy-start.9
  10.2 0.7 copy-start.10
  11.6 61.7 %copy-start.6 = (s32[256]{0:T(256)S(1)}, s32[256]{0:T(256)}, u32[]{:S(2)}) copy-start(s32[256]{0:T(256)} %param.10) | copy-start | bytes 3076
  11.7 61.7 %copy-start.8 = (s32[256]{0:T(256)S(1)}, s32[256]{0:T(256)}, u32[]{:S(2)}) copy-start(s32[256]{0:T(256)} %param.11) | copy-start | bytes 3076
  31.5 0.7 copy-start.5
  32.2 0.7 copy-start.7
  44.7 16.7 %all-to-all-start.2 = ((f32[16,1,2304]{2,1,0:T(1,128)}), f32[16,1,2304]{2,1,0:T(1,128)S(1)}, u32[]{:S(2)}, u32[]{:S(2)}) async-start(f32[16,1,2304]{2,1,0:T(1,128)} %bitcast.14), calls=%async_computation.2 | async-start | bytes 294912 | tf_op jit(solution)/shard_map/all_to_all | solution.py:330
  73.4 1.3 %copy-start = (f32[2368,128]{1,0:T(8,128)S(1)}, f32[2368,128]{1,0:T(8,128)}, u32[]{:S(2)}) copy-start(f32[2368,128]{1,0:T(8,128)} %all-gather.3.cloned.1.call-done) | copy-start | bytes 3637252
  74.7 28.8 %copy-start.1 = (f32[2368,128]{1,0:T(8,128)S(1)}, f32[2368,128]{1,0:T(8,128)}, u32[]{:S(2)}) copy-start(f32[2368,128]{1,0:T(8,128)} %all-gather.3.cloned.1.call-done) | copy-start | bytes 3637252
  78.0 13.2 %all-to-all-start.4 = ((f32[32,1,1152]{2,1,0:T(1,128)}), f32[32,1,1152]{2,1,0:T(1,128)S(1)}, u32[]{:S(2)}, u32[]{:S(2)}) async-start(f32[32,1,1152]{2,1,0:T(1,128)} %bitcast.19), calls=%async_computation.4 | async-start | bytes 294912 | tf_op jit(solution)/shard_map/all_to_all | solution.py:330
Sparse Core Ops, SparseCore 0:
  11.8 42.7 all-gather.2

commit v4 on v2

--- a/solution.py
+++ b/solution.py
@@ -50,23 +50,21 @@
 
 
 def select_sum(left, right, dims):
-    total = None
-    for part in halves(left):
-        term = lax.dot_general(
-            part, right, (dims, ((), ())), preferred_element_type=jnp.float32
-        )
-        total = term if total is None else total + term
-    return total
+    rows = left.shape[0]
+    both = lax.dot_general(
+        jnp.concatenate(halves(left), axis=0), right, (dims, ((), ())),
+        preferred_element_type=jnp.float32,
+    )
+    return both[:rows] + both[rows:]
 
 
 def pick_sum(left, right, dims):
-    total = None
-    for part in halves(right):
-        term = lax.dot_general(
-            left, part, (dims, ((), ())), preferred_element_type=jnp.float32
-        )
-        total = term if total is None else total + term
-    return total
+    rows = right.shape[0]
+    both = lax.dot_general(
+        left, jnp.concatenate(halves(right), axis=0), (dims, ((), ())),
+        preferred_element_type=jnp.float32,
+    )
+    return both[:, :rows] + both[:, rows:]
 
 
 def placed(station):
@@ -139,8 +137,9 @@
     curv = jnp.concatenate(curvs, axis=1)
     spread = jnp.concatenate([jnp.where(odd, 0.0, terms), jnp.where(odd, terms, 0.0)], axis=0)
     grads = pick_sum(hot, spread, ((1,), (1,)))
-    place = station % RUN
-    spread = jnp.concatenate([jnp.where(place == j, curv, 0.0) for j in range(RUN)], axis=0)
+    wide = jnp.concatenate([curv] * RUN, axis=0)
+    seat = lax.broadcasted_iota(jnp.int32, wide.shape, 0) // DIRS
+    spread = jnp.where(seat == station % RUN, wide, 0.0)
     rows = lax.broadcasted_iota(jnp.int32, (2 * pairs // RUN, 2 * base), 0)
     hot = jnp.where(rows == station // RUN, 1.0, 0.0).astype(jnp.bfloat16)
     curvs = pick_sum(hot, spread, ((1,), (1,)))
@@ -216,19 +215,18 @@
         copies_ref[at : at + RUN, :] = gains
 
 
-def last_kernel(at_ref, parts_ref, gains_ref, gains_out_ref, white_ref, rows_ref):
-    half = RUN // 2
-    source = lax.broadcasted_iota(jnp.int32, (half, RUN), 0)
-    target = lax.broadcasted_iota(jnp.int32, (half, RUN), 1)
-    for value, out_ref in zip(stepped(at_ref, parts_ref, gains_ref), (gains_out_ref, white_ref)):
-        rows_ref[...] = value
-        turned = rows_ref[pl.ds(pl.multiple_of(at_ref[1], half), half), :].T
+def last_kernel(at_ref, half_ref, parts_ref, gains_ref, gains_out_ref, white_ref):
+    owned = gains_out_ref.shape[1]
+    source = lax.broadcasted_iota(jnp.int32, (RUN, owned), 0) - half_ref[0]
+    target = lax.broadcasted_iota(jnp.int32, (RUN, owned), 1)
+    results = stepped(at_ref, parts_ref, gains_ref)
+    for value, out_ref in zip(results, (gains_out_ref, white_ref)):
         out = None
         for odd in range(2):
-            place = jnp.where(target == 2 * source + odd, 1.0, 0.0)
-            part = jnp.dot(
-                turned[odd * VALS : (odd + 1) * VALS],
-                place,
+            part = lax.dot_general(
+                value[:, odd * VALS : (odd + 1) * VALS],
+                jnp.where(target == 2 * source + odd, 1.0, 0.0),
+                (((0,), (0,)), ((), ())),
                 precision=lax.Precision.HIGHEST,
                 preferred_element_type=jnp.float32,
             )
@@ -248,17 +246,15 @@
     )(at, parts, gains)
 
 
-def last(at, parts, gains):
+def last(at, half, parts, gains, owned):
     return pl.pallas_call(
         last_kernel,
-        out_shape=(jax.ShapeDtypeStruct((VALS, RUN), jnp.float32),) * 2,
-        in_specs=[pl.BlockSpec(memory_space=pltpu.SMEM)]
-        + [pl.BlockSpec(memory_space=pltpu.VMEM)] * 2,
-        out_specs=(pl.BlockSpec(memory_space=pltpu.VMEM),) * 2,
-        scratch_shapes=[pltpu.VMEM((RUN, LANES), jnp.float32)],
+        out_shape=(jax.ShapeDtypeStruct((VALS, owned), jnp.float32),) * 2,
+        in_specs=[pl.BlockSpec(memory_space=pltpu.SMEM)] * 2 + [pl.BlockSpec(memory_space=pltpu.VMEM)] * 2,
+        out_specs=tuple([pl.BlockSpec(memory_space=pltpu.VMEM)] * 2),
         compiler_params=pltpu.CompilerParams(vmem_limit_bytes=16 * 2**20),
         name="last",
-    )(at, parts, gains)
+    )(at, half, parts, gains)
 
 
 def exchange(rows, axes, peers):
@@ -271,22 +267,22 @@
     base = antenna1.shape[0]
     channels = model.shape[1]
     owned = gains.shape[3]
-    near, far = ("x", "z0", "core"), ("y", "z1")
+    near, far = ("x", "z0", "core"), ("z1", "y")
     model = model.reshape(channels, VALS, base)
     vis, weights = vis[0], weights[0]
     first, second, live = (a.reshape(1, base) for a in (antenna1, antenna2, live))
     mine = gains.reshape(VALS, owned).T.reshape(1, owned * VALS // LANES, LANES)
     mine = jnp.broadcast_to(mine, (32,) + mine.shape[1:]).reshape(-1, LANES)
     full = exchange(mine, near + ("z1",), 32)
-    place = lax.axis_index(near)
-    at = jnp.stack([place * RUN, lax.axis_index("z1") * (RUN // 2)]).astype(jnp.int32)
+    at = (lax.axis_index(near) * RUN).reshape(1).astype(jnp.int32)
+    half = (lax.axis_index("z1") * (RUN // 2)).reshape(1).astype(jnp.int32)
     for turn in range(ITERS):
         sent = partials(full, model, vis, weights, live, first, second)
         sent = total(exchange(sent, near, 16), 16)
         sums = exchange(sent, far, 16)
         if turn < ITERS - 1:
             full = exchange(step(at, sums, full, 16), near, 16)
-    return tuple(out.reshape(gains.shape) for out in last(at, sums, full))
+    return tuple(out.reshape(gains.shape) for out in last(at, half, sums, full, owned))
 
 
 def solution(mesh):

time: 121 us -> 118 us (0.975)
  blocking collectives: 94.4 us -> 81.4 us
  waiting for transfers between devices: 9.42 us -> 16.6 us
  starting transfers between devices: 7.14 us -> 10.7 us
    all_to_all x8 -> x7, blocking collectives: 94.4 us -> 81.4 us  [exchange(): return lax.all_to_all(sent, axes, 0, 0).reshape(count, LANES)]
    all_to_all x1 -> x2, waiting for transfers between devices: 9.42 us -> 16.6 us  [exchange(): return lax.all_to_all(sent, axes, 0, 0).reshape(count, LANES)]
    all_to_all x1 -> x2, starting transfers between devices: 7.14 us -> 10.7 us  [exchange(): return lax.all_to_all(sent, axes, 0, 0).reshape(count, LANES)]
  transfers between devices with their start and end apart: 1 -> 2, of which waited for: 1 -> 2; matrix products, arithmetic and copies ran while one was open for 0% -> 0% of each run, Pallas kernels for 0% -> 0%
where the time goes in v4:
time: 118 us; the launch traced here: 117 us
  blocking collectives  81.4 us (69%)
  waiting for transfers between devices  16.6 us (14%)
  starting transfers between devices  10.7 us (9%)
  Pallas kernels  5.55 us (5%)
  local copies, waits for them, and re-layouts  1.68 us (1%)
    all_to_all x7, blocking collectives, exchange(): return lax.all_to_all(sent, axes, 0, 0).reshape(count, LANES)  81.4 us
    all_to_all x2, waiting for transfers between devices, exchange(): return lax.all_to_all(sent, axes, 0, 0).reshape(count, LANES)  16.6 us
    all_to_all x2, starting transfers between devices, exchange(): return lax.all_to_all(sent, axes, 0, 0).reshape(count, LANES)  10.7 us
    pallas_call x3, Pallas kernels, partials(): pl.pallas_call(partials_kernel, out_shape=jax.ShapeDtypeStruct((pairs //...  2.6 us
  transfers between devices with their start and end apart: 2, of which 2 were waited for; matrix products, arithmetic and copies ran while one was open for 0% of the time, Pallas kernels for 0%

profile of v4, /device:TPU:1, one launch (start us, length us, event | category | flops | bytes accessed | tf_op | source)
XLA Modules:
  0.0 116.6 jit_solution(16956095876001799439)
XLA Ops:
  0.6 0.8 copy.10
  1.4 0.1 broadcast_in_dim.7
  1.5 0.1 broadcast_in_dim.8
  1.6 0.0 copy-start
  1.6 0.0 copy-start.1
  1.6 20.0 %all_to_all.45 = f32[32,1,1024]{2,1,0:T(1,128)S(1)} all-to-all(f32[32,1,1024]{2,1,0:T(1,128)S(1)} %broadcast_in_dim.8), channel_id=1, replica_groups=mesh['y'=8,'x'=4,'z1'=2,'z0'=2,'core'=2,'chan'=2] {'x','z0','core','z1'}, dimensions={0} | all-to-all | bytes 262144 | tf_op jit(solution)/shard_map/all_to_all | solution.py:263
  21.6 0.0 copy-start.4
  21.6 0.0 copy-start.5
  21.6 0.0 copy-start.2
  21.6 0.0 copy-start.3
  21.6 0.0 copy-done
  21.6 0.0 copy-done.1
  21.7 0.6 copy-done.4
  22.3 0.0 copy-done.5
  22.3 0.0 copy-done.2
  22.3 0.0 copy-done.3
  22.3 0.9 partials.3
  23.2 9.3 %all_to_all.46 = f32[16,1,2304]{2,1,0:T(1,128)S(1)} all-to-all(f32[16,1,2304]{2,1,0:T(1,128)S(1)} %bitcast.42), channel_id=1, replica_groups=mesh['y'=8,'x'=4,'z1'=2,'z0'=2,'core'=2,'chan'=2] {'x','z0','core'}, dimensions={0} | all-to-all | bytes 294912 | tf_op jit(solution)/shard_map/all_to_all | solution.py:263
  32.5 0.7 total.3
  33.2 7.1 %all-to-all-start.2 = ((f32[16,1,2304]{2,1,0:T(1,128)}), f32[16,1,2304]{2,1,0:T(1,128)S(1)}, u32[]{:S(2)}, u32[]{:S(2)}) async-start(f32[16,1,2304]{2,1,0:T(1,128)} %bitcast.13), calls=%async_computation.2 | async-start | bytes 294912 | tf_op jit(solution)/shard_map/all_to_all | solution.py:263
  40.4 8.3 %all-to-all-done.2 = f32[16,1,2304]{2,1,0:T(1,128)S(1)} async-done(((f32[16,1,2304]{2,1,0:T(1,128)}), f32[16,1,2304]{2,1,0:T(1,128)S(1)}, u32[]{:S(2)}, u32[]{:S(2)}) %all-to-all-start.2) | async-done | bytes 147488 | tf_op jit(solution)/shard_map/all_to_all | solution.py:263
  48.7 0.2 step.2
  48.9 10.9 %all_to_all.47 = f32[16,1,2048]{2,1,0:T(1,128)S(1)} all-to-all(f32[16,1,2048]{2,1,0:T(1,128)S(1)} %bitcast.48), channel_id=1, replica_groups=mesh['y'=8,'x'=4,'z1'=2,'z0'=2,'core'=2,'chan'=2] {'x','z0','core'}, dimensions={0} | all-to-all | bytes 262144 | tf_op jit(solution)/shard_map/all_to_all | solution.py:263
  59.8 0.9 partials.4
  60.7 9.4 %all_to_all.48 = f32[16,1,2304]{2,1,0:T(1,128)S(1)} all-to-all(f32[16,1,2304]{2,1,0:T(1,128)S(1)} %bitcast.43), channel_id=1, replica_groups=mesh['y'=8,'x'=4,'z1'=2,'z0'=2,'core'=2,'chan'=2] {'x','z0','core'}, dimensions={0} | all-to-all | bytes 294912 | tf_op jit(solution)/shard_map/all_to_all | solution.py:263
  70.2 11.3 %all_to_all.49 = f32[16,1,2304]{2,1,0:T(1,128)S(1)} all-to-all(f32[16,1,2304]{2,1,0:T(1,128)S(1)} %bitcast.40), channel_id=1, replica_groups=mesh['y'=8,'x'=4,'z1'=2,'z0'=2,'core'=2,'chan'=2] {'z1','y'}, dimensions={0} | all-to-all | bytes 294912 | tf_op jit(solution)/shard_map/all_to_all | solution.py:263
  81.5 0.2 step.3
  81.7 10.9 %all_to_all.50 = f32[16,1,2048]{2,1,0:T(1,128)S(1)} all-to-all(f32[16,1,2048]{2,1,0:T(1,128)S(1)} %bitcast.49), channel_id=1, replica_groups=mesh['y'=8,'x'=4,'z1'=2,'z0'=2,'core'=2,'chan'=2] {'x','z0','core'}, dimensions={0} | all-to-all | bytes 262144 | tf_op jit(solution)/shard_map/all_to_all | solution.py:263
  92.6 0.9 partials.5
  93.5 9.4 %all_to_all.51 = f32[16,1,2304]{2,1,0:T(1,128)S(1)} all-to-all(f32[16,1,2304]{2,1,0:T(1,128)S(1)} %bitcast.44), channel_id=1, replica_groups=mesh['y'=8,'x'=4,'z1'=2,'z0'=2,'core'=2,'chan'=2] {'x','z0','core'}, dimensions={0} | all-to-all | bytes 294912 | tf_op jit(solution)/shard_map/all_to_all | solution.py:263
  103.0 0.7 total.5
  103.6 3.5 %all-to-all-start.8 = ((f32[16,1,2304]{2,1,0:T(1,128)}), f32[16,1,2304]{2,1,0:T(1,128)S(1)}, u32[]{:S(2)}, u32[]{:S(2)}) async-start(f32[16,1,2304]{2,1,0:T(1,128)} %bitcast.25), calls=%async_computation.8 | async-start | bytes 294912 | tf_op jit(solution)/shard_map/all_to_all | solution.py:263
  107.2 8.3 %all-to-all-done.8 = f32[16,1,2304]{2,1,0:T(1,128)S(1)} async-done(((f32[16,1,2304]{2,1,0:T(1,128)}), f32[16,1,2304]{2,1,0:T(1,128)S(1)}, u32[]{:S(2)}, u32[]{:S(2)}) %all-to-all-start.8) | async-done | bytes 147488 | tf_op jit(solution)/shard_map/all_to_all | solution.py:263
  115.5 1.2 %last.1 = (f32[64,16]{1,0:T(8,128)}, f32[64,16]{1,0:T(8,128)}) custom-call(s32[1]{0:T(128)} %bitcast.at_ref, s32[1]{0:T(128)} %bitcast.1.half_ref, f32[288,128]{1,0:T(8,128)S(1)} %bitcast.36, f32[256,128]{1,0:T(8,128)S(1)} %bitcast.32), custom_call_target="tpu_custom_call" | custom-call | tf_op jit(solution)/shard_map/last/pallas_call | solution.py:250
  (1 shorter events, 0.0 us)
Async XLA Ops:
  1.6 20.0 %copy-start = (bf16[1,2,8,8,256]{4,3,2,1,0:T(8,128)(2,1)S(1)}, bf16[1,2,8,8,256]{4,3,2,1,0:T(8,128)(2,1)}, u32[]{:S(2)}) copy-start(bf16[1,2,8,8,256]{4,3,2,1,0:T(8,128)(2,1)} %param.7) | copy-start | bytes 196612
  1.6 20.0 %copy-start.1 = (f32[1,2,8,256]{3,2,1,0:T(8,128)S(1)}, f32[1,2,8,256]{3,2,1,0:T(8,128)}, u32[]{:S(2)}) copy-start(f32[1,2,8,256]{3,2,1,0:T(8,128)} %param.8) | copy-start | bytes 49156
  21.6 0.7 copy-start.4
  21.6 0.7 copy-start.5
  21.6 0.7 copy-start.2
  21.6 0.7 copy-start.3
  33.2 15.5 %all-to-all-start.2 = ((f32[16,1,2304]{2,1,0:T(1,128)}), f32[16,1,2304]{2,1,0:T(1,128)S(1)}, u32[]{:S(2)}, u32[]{:S(2)}) async-start(f32[16,1,2304]{2,1,0:T(1,128)} %bitcast.13), calls=%async_computation.2 | async-start | bytes 294912 | tf_op jit(solution)/shard_map/all_to_all | solution.py:263
  103.6 11.8 %all-to-all-start.8 = ((f32[16,1,2304]{2,1,0:T(1,128)}), f32[16,1,2304]{2,1,0:T(1,128)S(1)}, u32[]{:S(2)}, u32[]{:S(2)}) async-start(f32[16,1,2304]{2,1,0:T(1,128)} %bitcast.25), calls=%async_computation.8 | async-start | bytes 294912 | tf_op jit(solution)/shard_map/all_to_all | solution.py:263

commit v5 on v4

--- a/solution.py
+++ b/solution.py
@@ -15,6 +15,8 @@
 VALS = DIRS * COMPS
 LANES = 128
 RUN = LANES // DIRS
+NEAR = ("x", "z0", "core")
+FAR = ("z1", "y")
 
 
 def cmul(left, right):
@@ -192,7 +194,7 @@
     )(parts)
 
 
-def stepped(at_ref, parts_ref, gains_ref):
+def stepped(parts_ref, gains_ref):
     sums = peers_sum(parts_ref, RUN + 2)
     grad = sums[:RUN]
     row = lax.broadcasted_iota(jnp.int32, (RUN, LANES), 0)
@@ -205,21 +207,23 @@
     denom = 1.0 + jnp.dot(
         curv, wide, precision=lax.Precision.HIGHEST, preferred_element_type=jnp.float32
     )
-    old = gains_ref[pl.ds(pl.multiple_of(at_ref[0], RUN), RUN), :]
+    at = lax.axis_index(NEAR) * RUN
+    old = gains_ref[pl.ds(pl.multiple_of(at, RUN), RUN), :]
     return old - STEP * grad / denom, grad / jnp.sqrt(denom)
 
 
-def step_kernel(at_ref, parts_ref, gains_ref, copies_ref):
-    gains, _ = stepped(at_ref, parts_ref, gains_ref)
+def step_kernel(parts_ref, gains_ref, copies_ref):
+    gains, _ = stepped(parts_ref, gains_ref)
     for at in range(0, copies_ref.shape[0], RUN):
         copies_ref[at : at + RUN, :] = gains
 
 
-def last_kernel(at_ref, half_ref, parts_ref, gains_ref, gains_out_ref, white_ref):
+def last_kernel(parts_ref, gains_ref, gains_out_ref, white_ref):
     owned = gains_out_ref.shape[1]
-    source = lax.broadcasted_iota(jnp.int32, (RUN, owned), 0) - half_ref[0]
+    first = lax.axis_index("z1") * (RUN // 2)
+    source = lax.broadcasted_iota(jnp.int32, (RUN, owned), 0) - first
     target = lax.broadcasted_iota(jnp.int32, (RUN, owned), 1)
-    results = stepped(at_ref, parts_ref, gains_ref)
+    results = stepped(parts_ref, gains_ref)
     for value, out_ref in zip(results, (gains_out_ref, white_ref)):
         out = None
         for odd in range(2):
@@ -234,27 +238,26 @@
         out_ref[...] = out
 
 
-def step(at, parts, gains, peers):
+def step(parts, gains, peers):
     return pl.pallas_call(
         step_kernel,
         out_shape=jax.ShapeDtypeStruct((peers * RUN, LANES), jnp.float32),
-        in_specs=[pl.BlockSpec(memory_space=pltpu.SMEM)]
-        + [pl.BlockSpec(memory_space=pltpu.VMEM)] * 2,
+        in_specs=[pl.BlockSpec(memory_space=pltpu.VMEM)] * 2,
         out_specs=pl.BlockSpec(memory_space=pltpu.VMEM),
         compiler_params=pltpu.CompilerParams(vmem_limit_bytes=16 * 2**20),
         name="step",
-    )(at, parts, gains)
-
-
-def last(at, half, parts, gains, owned):
+    )(parts, gains)
+
+
+def last(parts, gains, owned):
     return pl.pallas_call(
         last_kernel,
         out_shape=(jax.ShapeDtypeStruct((VALS, owned), jnp.float32),) * 2,
-        in_specs=[pl.BlockSpec(memory_space=pltpu.SMEM)] * 2 + [pl.BlockSpec(memory_space=pltpu.VMEM)] * 2,
+        in_specs=[pl.BlockSpec(memory_space=pltpu.VMEM)] * 2,
         out_specs=tuple([pl.BlockSpec(memory_space=pltpu.VMEM)] * 2),
         compiler_params=pltpu.CompilerParams(vmem_limit_bytes=16 * 2**20),
         name="last",
-    )(at, half, parts, gains)
+    )(parts, gains)
 
 
 def exchange(rows, axes, peers):
@@ -267,22 +270,19 @@
     base = antenna1.shape[0]
     channels = model.shape[1]
     owned = gains.shape[3]
-    near, far = ("x", "z0", "core"), ("z1", "y")
     model = model.reshape(channels, VALS, base)
     vis, weights = vis[0], weights[0]
     first, second, live = (a.reshape(1, base) for a in (antenna1, antenna2, live))
     mine = gains.reshape(VALS, owned).T.reshape(1, owned * VALS // LANES, LANES)
     mine = jnp.broadcast_to(mine, (32,) + mine.shape[1:]).reshape(-1, LANES)
-    full = exchange(mine, near + ("z1",), 32)
-    at = (lax.axis_index(near) * RUN).reshape(1).astype(jnp.int32)
-    half = (lax.axis_index("z1") * (RUN // 2)).reshape(1).astype(jnp.int32)
+    full = exchange(mine, NEAR + ("z1",), 32)
     for turn in range(ITERS):
         sent = partials(full, model, vis, weights, live, first, second)
-        sent = total(exchange(sent, near, 16), 16)
-        sums = exchange(sent, far, 16)
+        sent = total(exchange(sent, NEAR, 16), 16)
+        sums = exchange(sent, FAR, 16)
         if turn < ITERS - 1:
-            full = exchange(step(at, sums, full, 16), near, 16)
-    return tuple(out.reshape(gains.shape) for out in last(at, half, sums, full, owned))
+            full = exchange(step(sums, full, 16), NEAR, 16)
+    return tuple(out.reshape(gains.shape) for out in last(sums, full, owned))
 
 
 def solution(mesh):

time: 118 us -> 116 us (0.983)
  blocking collectives: 81.4 us -> 108 us
  waiting for transfers between devices: 16.6 us -> 0 us
  starting transfers between devices: 10.7 us -> 0 us
  Pallas kernels: 5.55 us -> 4.25 us
    all_to_all x7 -> x9, blocking collectives: 81.4 us -> 108 us  [exchange(): return lax.all_to_all(sent, axes, 0, 0).reshape(count, LANES)]
    all_to_all x2 -> x0, waiting for transfers between devices: 16.6 us -> none  [exchange(): return lax.all_to_all(sent, axes, 0, 0).reshape(count, LANES)]
    all_to_all x2 -> x0, starting transfers between devices: 10.7 us -> none  [exchange(): return lax.all_to_all(sent, axes, 0, 0).reshape(count, LANES)]
    pallas_call x3, Pallas kernels: 1.39 us -> 0.09 us  [total(): pl.pallas_call(total_kernel, out_shape=jax.ShapeDtypeStruct((peers * (RUN...]
  transfers between devices with their start and end apart: 2 -> 0, of which waited for: 2 -> 0; matrix products, arithmetic and copies ran while one was open for 0% -> 0% of each run, Pallas kernels for 0% -> 0%
where the time goes in v5:
time: 116 us; the launch traced here: 115 us
  blocking collectives  108 us (93%)
  Pallas kernels  4.25 us (4%)
  local copies, waits for them, and re-layouts  1.68 us (1%)
    all_to_all x9, blocking collectives, exchange(): return lax.all_to_all(sent, axes, 0, 0).reshape(count, LANES)  108 us
    pallas_call x3, Pallas kernels, partials(): pl.pallas_call(partials_kernel, out_shape=jax.ShapeDtypeStruct((pairs //...  2.6 us

profile of v5, /device:TPU:1, one launch (start us, length us, event | category | flops | bytes accessed | tf_op | source)
XLA Modules:
  0.0 114.7 jit_solution(6148938098400447936)
XLA Ops:
  0.6 0.8 copy.10
  1.4 0.1 broadcast_in_dim.7
  1.5 0.1 broadcast_in_dim.8
  1.6 0.0 copy-start
  1.6 0.0 copy-start.1
  1.6 20.0 %all_to_all.45 = f32[32,1,1024]{2,1,0:T(1,128)S(1)} all-to-all(f32[32,1,1024]{2,1,0:T(1,128)S(1)} %broadcast_in_dim.8), channel_id=1, replica_groups=mesh['y'=8,'x'=4,'z1'=2,'z0'=2,'core'=2,'chan'=2] {'x','z0','core','z1'}, dimensions={0} | all-to-all | bytes 262144 | tf_op jit(solution)/shard_map/all_to_all | solution.py:266
  21.6 0.0 copy-start.4
  21.6 0.0 copy-start.5
  21.6 0.0 copy-start.2
  21.6 0.0 copy-start.3
  21.6 0.0 copy-done
  21.6 0.0 copy-done.1
  21.7 0.6 copy-done.4
  22.3 0.0 copy-done.5
  22.3 0.0 copy-done.2
  22.3 0.0 copy-done.3
  22.3 0.9 partials.3
  23.2 9.3 %all_to_all.46 = f32[16,1,2304]{2,1,0:T(1,128)S(1)} all-to-all(f32[16,1,2304]{2,1,0:T(1,128)S(1)} %bitcast.42), channel_id=1, replica_groups=mesh['y'=8,'x'=4,'z1'=2,'z0'=2,'core'=2,'chan'=2] {'x','z0','core'}, dimensions={0} | all-to-all | bytes 294912 | tf_op jit(solution)/shard_map/all_to_all | solution.py:266
  32.6 15.3 %all_to_all.47 = f32[16,1,2304]{2,1,0:T(1,128)S(1)} all-to-all(f32[16,1,2304]{2,1,0:T(1,128)S(1)} %bitcast.37), channel_id=1, replica_groups=mesh['y'=8,'x'=4,'z1'=2,'z0'=2,'core'=2,'chan'=2] {'z1','y'}, dimensions={0} | all-to-all | bytes 294912 | tf_op jit(solution)/shard_map/all_to_all | solution.py:266
  47.8 0.2 step.2
  48.0 10.9 %all_to_all.48 = f32[16,1,2048]{2,1,0:T(1,128)S(1)} all-to-all(f32[16,1,2048]{2,1,0:T(1,128)S(1)} %bitcast.48), channel_id=1, replica_groups=mesh['y'=8,'x'=4,'z1'=2,'z0'=2,'core'=2,'chan'=2] {'x','z0','core'}, dimensions={0} | all-to-all | bytes 262144 | tf_op jit(solution)/shard_map/all_to_all | solution.py:266
  59.0 0.9 partials.4
  59.8 9.4 %all_to_all.49 = f32[16,1,2304]{2,1,0:T(1,128)S(1)} all-to-all(f32[16,1,2304]{2,1,0:T(1,128)S(1)} %bitcast.43), channel_id=1, replica_groups=mesh['y'=8,'x'=4,'z1'=2,'z0'=2,'core'=2,'chan'=2] {'x','z0','core'}, dimensions={0} | all-to-all | bytes 294912 | tf_op jit(solution)/shard_map/all_to_all | solution.py:266
  69.3 11.3 %all_to_all.50 = f32[16,1,2304]{2,1,0:T(1,128)S(1)} all-to-all(f32[16,1,2304]{2,1,0:T(1,128)S(1)} %bitcast.39), channel_id=1, replica_groups=mesh['y'=8,'x'=4,'z1'=2,'z0'=2,'core'=2,'chan'=2] {'z1','y'}, dimensions={0} | all-to-all | bytes 294912 | tf_op jit(solution)/shard_map/all_to_all | solution.py:266
  80.7 0.2 step.3
  80.9 10.9 %all_to_all.51 = f32[16,1,2048]{2,1,0:T(1,128)S(1)} all-to-all(f32[16,1,2048]{2,1,0:T(1,128)S(1)} %bitcast.49), channel_id=1, replica_groups=mesh['y'=8,'x'=4,'z1'=2,'z0'=2,'core'=2,'chan'=2] {'x','z0','core'}, dimensions={0} | all-to-all | bytes 262144 | tf_op jit(solution)/shard_map/all_to_all | solution.py:266
  91.8 0.9 partials.5
  92.7 9.4 %all_to_all.52 = f32[16,1,2304]{2,1,0:T(1,128)S(1)} all-to-all(f32[16,1,2304]{2,1,0:T(1,128)S(1)} %bitcast.44), channel_id=1, replica_groups=mesh['y'=8,'x'=4,'z1'=2,'z0'=2,'core'=2,'chan'=2] {'x','z0','core'}, dimensions={0} | all-to-all | bytes 294912 | tf_op jit(solution)/shard_map/all_to_all | solution.py:266
  102.1 11.4 %all_to_all.53 = f32[16,1,2304]{2,1,0:T(1,128)S(1)} all-to-all(f32[16,1,2304]{2,1,0:T(1,128)S(1)} %bitcast.41), channel_id=1, replica_groups=mesh['y'=8,'x'=4,'z1'=2,'z0'=2,'core'=2,'chan'=2] {'z1','y'}, dimensions={0} | all-to-all | bytes 294912 | tf_op jit(solution)/shard_map/all_to_all | solution.py:266
  113.5 1.2 %last.1 = (f32[64,16]{1,0:T(8,128)}, f32[64,16]{1,0:T(8,128)}) custom-call(f32[288,128]{1,0:T(8,128)S(1)} %bitcast.35, f32[256,128]{1,0:T(8,128)S(1)} %bitcast.32), custom_call_target="tpu_custom_call" | custom-call | tf_op jit(solution)/shard_map/last/pallas_call | solution.py:253
  (3 shorter events, 0.1 us)
Async XLA Ops:
  1.6 20.0 %copy-start = (bf16[1,2,8,8,256]{4,3,2,1,0:T(8,128)(2,1)S(1)}, bf16[1,2,8,8,256]{4,3,2,1,0:T(8,128)(2,1)}, u32[]{:S(2)}) copy-start(bf16[1,2,8,8,256]{4,3,2,1,0:T(8,128)(2,1)} %param.7) | copy-start | bytes 196612
  1.6 20.0 %copy-start.1 = (f32[1,2,8,256]{3,2,1,0:T(8,128)S(1)}, f32[1,2,8,256]{3,2,1,0:T(8,128)}, u32[]{:S(2)}) copy-start(f32[1,2,8,256]{3,2,1,0:T(8,128)} %param.8) | copy-start | bytes 49156
  21.6 0.7 copy-start.4
  21.6 0.7 copy-start.5
  21.6 0.7 copy-start.2
  21.6 0.7 copy-start.3

commit v6 on v3

--- a/solution.py
+++ b/solution.py
@@ -15,6 +15,9 @@
 VALS = DIRS * COMPS
 LANES = 128
 RUN = LANES // DIRS
+NEAR = ("x", "z0", "core")
+FAR = ("z1", "y")
+WIDE = NEAR + ("z1",)
 
 
 def cmul(left, right):
@@ -50,23 +53,21 @@
 
 
 def select_sum(left, right, dims):
-    total = None
-    for part in halves(left):
-        term = lax.dot_general(
-            part, right, (dims, ((), ())), preferred_element_type=jnp.float32
-        )
-        total = term if total is None else total + term
-    return total
+    rows = left.shape[0]
+    both = lax.dot_general(
+        jnp.concatenate(halves(left), axis=0), right, (dims, ((), ())),
+        preferred_element_type=jnp.float32,
+    )
+    return both[:rows] + both[rows:]
 
 
 def pick_sum(left, right, dims):
-    total = None
-    for part in halves(right):
-        term = lax.dot_general(
-            left, part, (dims, ((), ())), preferred_element_type=jnp.float32
-        )
-        total = term if total is None else total + term
-    return total
+    rows = right.shape[0]
+    both = lax.dot_general(
+        left, jnp.concatenate(halves(right), axis=0), (dims, ((), ())),
+        preferred_element_type=jnp.float32,
+    )
+    return both[:, :rows] + both[:, rows:]
 
 
 def placed(station):
@@ -81,23 +82,22 @@
 PARAMS = pltpu.CompilerParams(vmem_limit_bytes=16 * 2**20)
 
 
-def pack_kernel(model_ref, vis_ref, weight_ref, live_ref, gains_ref, data_ref, copies_ref):
-    channels, base = weight_ref.shape
-    cuts = base // LANES
-    live = live_ref[...].astype(jnp.float32)
-    scales = []
-    for part in range(channels * cuts):
-        channel, cut = divmod(part, cuts)
-        lanes = slice(cut * LANES, (cut + 1) * LANES)
-        at = part * (VALS + COMPS)
-        data_ref[at : at + VALS, :] = model_ref[channel, :, lanes].astype(jnp.float32)
-        data_ref[at + VALS : at + VALS + COMPS, :] = vis_ref[channel, :, lanes]
-        scales.append(weight_ref[channel : channel + 1, lanes] * live[:, lanes])
-    at = len(scales) * (VALS + COMPS)
-    spare = data_ref.shape[0] - at - len(scales)
-    scales.append(jnp.zeros((spare, LANES), jnp.float32))
-    data_ref[at:, :] = jnp.concatenate(scales, axis=0)
-
+def pack_kernel(
+    model_hbm, vis_hbm, weight_hbm, live_hbm, first_hbm, second_hbm, gains_hbm,
+    data_ref, own_ref, copies_ref,
+    model_ref, vis_ref, weight_ref, live_ref, first_ref, second_ref, gains_ref, sems,
+):
+    pairs = (
+        (gains_hbm, gains_ref), (model_hbm, model_ref), (vis_hbm, vis_ref), (weight_hbm, weight_ref),
+        (live_hbm, live_ref), (first_hbm, first_ref), (second_hbm, second_ref),
+    )
+    moves = [
+        pltpu.make_async_copy(source, target, sems.at[index])
+        for index, (source, target) in enumerate(pairs)
+    ]
+    for move in moves:
+        move.start()
+    moves[0].wait()
     owned = gains_ref.shape[1]
     target = lax.broadcasted_iota(jnp.int32, (owned // 2, owned), 0)
     source = lax.broadcasted_iota(jnp.int32, (owned // 2, owned), 1)
@@ -116,34 +116,59 @@
     )
     for at in range(0, copies_ref.shape[0], owned // 2):
         copies_ref[at : at + owned // 2, :] = mine
-
-
-def pack(model, vis, weights, live, gains, peers):
+    for move in moves[1:]:
+        move.wait()
+
+    channels, base = weight_ref.shape
+    cuts = base // LANES
+    live = live_ref[...].astype(jnp.float32)
+    tail = []
+    for part in range(channels * cuts):
+        channel, cut = divmod(part, cuts)
+        lanes = slice(cut * LANES, (cut + 1) * LANES)
+        at = part * (VALS + COMPS)
+        for ref in (data_ref, own_ref):
+            ref[at : at + VALS, :] = model_ref[channel, :, lanes].astype(jnp.float32)
+            ref[at + VALS : at + VALS + COMPS, :] = vis_ref[channel, :, lanes]
+        tail.append(weight_ref[channel : channel + 1, lanes] * live[:, lanes])
+    for station_ref in (first_ref, second_ref):
+        station = station_ref[...].astype(jnp.float32)
+        tail += [station[:, cut * LANES : (cut + 1) * LANES] for cut in range(cuts)]
+    for ref in (data_ref, own_ref):
+        ref[channels * cuts * (VALS + COMPS) :, :] = jnp.concatenate(tail, axis=0)
+
+
+def pack(model, vis, weights, live, first, second, gains, peers):
     channels, base = weights.shape
-    parts = channels * base // LANES
-    rows = parts * (VALS + COMPS) + -(-parts // 8) * 8
-    owned = gains.shape[1]
+    cuts = base // LANES
+    rows = channels * cuts * (VALS + COMPS + 1) + 2 * cuts
+    args = (model, vis, weights, live, first, second, gains)
     return pl.pallas_call(
         pack_kernel,
         out_shape=(
             jax.ShapeDtypeStruct((rows, LANES), jnp.float32),
-            jax.ShapeDtypeStruct((peers * owned // 2, LANES), jnp.float32),
+            jax.ShapeDtypeStruct((rows, LANES), jnp.float32),
+            jax.ShapeDtypeStruct((peers * gains.shape[1] // 2, LANES), jnp.float32),
         ),
-        in_specs=in_vmem(5),
-        out_specs=tuple(in_vmem(2)),
-        compiler_params=PARAMS,
+        in_specs=[pl.BlockSpec(memory_space=pltpu.HBM)] * len(args),
+        out_specs=tuple(in_vmem(3)),
+        scratch_shapes=[pltpu.VMEM(a.shape, a.dtype) for a in args]
+        + [pltpu.SemaphoreType.DMA((len(args),))],
+        compiler_params=pltpu.CompilerParams(vmem_limit_bytes=63 * 2**20),
         name="pack",
-    )(model, vis, weights, live, gains)
+    )(*args)
 
 
 def partials_kernel(
-    run, channels, gains_ref, data_ref, first_ref, second_ref, out_ref, picked_ref, terms_ref
+    run, channels, gains_ref, data_ref, out_ref, picked_ref, terms_ref
 ):
-    base = first_ref.shape[1]
     pairs = gains_ref.shape[0]
     times = data_ref.shape[0]
-    cuts = base // LANES
-    station = placed(jnp.concatenate([first_ref[...], second_ref[...]], axis=1))
+    cuts = picked_ref.shape[0] // 2
+    base = cuts * LANES
+    tail = channels * cuts * (VALS + COMPS + 1)
+    ends = [data_ref[0, tail + end : tail + end + 1, :] for end in range(2 * cuts)]
+    station = placed(jnp.concatenate(ends, axis=1).astype(jnp.int32))
     rows = lax.broadcasted_iota(jnp.int32, (pairs, 2 * base), 0)
     hot = jnp.where(rows == station // 2, 1.0, 0.0).astype(jnp.bfloat16)
     odd = station % 2 == 1
@@ -193,8 +218,8 @@
             return totals
 
         totals = at_time(0, None)
-        if times > 1:
-            totals = lax.fori_loop(1, times, at_time, totals)
+        for time in range(1, times):
+            totals = at_time(time, totals)
         for side in range(2):
             at = side * cuts + cut
             for index, (real, imag) in enumerate(totals[side]):
@@ -206,8 +231,9 @@
     curv = jnp.concatenate(curvs, axis=1)
     spread = jnp.concatenate([jnp.where(odd, 0.0, terms), jnp.where(odd, terms, 0.0)], axis=0)
     grads = pick_sum(hot, spread, ((1,), (1,)))
-    place = station % RUN
-    spread = jnp.concatenate([jnp.where(place == j, curv, 0.0) for j in range(RUN)], axis=0)
+    wide = jnp.concatenate([curv] * RUN, axis=0)
+    seat = lax.broadcasted_iota(jnp.int32, wide.shape, 0) // DIRS
+    spread = jnp.where(seat == station % RUN, wide, 0.0)
     rows = lax.broadcasted_iota(jnp.int32, (2 * pairs // RUN, 2 * base), 0)
     hot = jnp.where(rows == station // RUN, 1.0, 0.0).astype(jnp.bfloat16)
     curvs = pick_sum(hot, spread, ((1,), (1,)))
@@ -218,18 +244,18 @@
         out_ref[at + run : at + run + extra, :] = curvs[peer * extra : (peer + 1) * extra]
 
 
-def partials(run, channels, gains, data, first, second):
+def partials(run, channels, gains, data):
     pairs = gains.shape[0]
-    base = first.shape[1]
+    cuts = data.shape[1] // (channels * (VALS + COMPS + 1) + 2)
     return pl.pallas_call(
         functools.partial(partials_kernel, run, channels),
         out_shape=jax.ShapeDtypeStruct((pairs // 8 * 9, LANES), jnp.float32),
-        in_specs=in_vmem(4),
+        in_specs=in_vmem(2),
         out_specs=in_vmem(1)[0],
-        scratch_shapes=[pltpu.VMEM((2 * base // LANES, VALS, LANES), jnp.float32)] * 2,
+        scratch_shapes=[pltpu.VMEM((2 * cuts, VALS, LANES), jnp.float32)] * 2,
         compiler_params=PARAMS,
         name="partials",
-    )(gains, data, first, second)
+    )(gains, data)
 
 
 def peers_sum(parts_ref, rows):
@@ -257,7 +283,7 @@
     )(parts)
 
 
-def stepped(run, at_ref, parts_ref, gains_ref):
+def stepped(run, parts_ref, gains_ref):
     sums = peers_sum(parts_ref, run // 8 * 9)
     grad = sums[:run]
     row = lax.broadcasted_iota(jnp.int32, (run, LANES), 0)
@@ -272,29 +298,29 @@
     denom = 1.0 + jnp.dot(
         curv, wide, precision=lax.Precision.HIGHEST, preferred_element_type=jnp.float32
     )
-    old = gains_ref[pl.ds(pl.multiple_of(at_ref[0], run), run), :]
+    at = lax.axis_index(NEAR if run == RUN else WIDE) * run
+    old = gains_ref[pl.ds(pl.multiple_of(at, run), run), :]
     return old - STEP * grad / denom, grad / jnp.sqrt(denom)
 
 
-def step_kernel(run, at_ref, parts_ref, gains_ref, copies_ref):
-    gains, _ = stepped(run, at_ref, parts_ref, gains_ref)
+def step_kernel(run, parts_ref, gains_ref, copies_ref):
+    gains, _ = stepped(run, parts_ref, gains_ref)
     for at in range(0, copies_ref.shape[0], run):
         copies_ref[at : at + run, :] = gains
 
 
-def last_kernel(run, at_ref, parts_ref, gains_ref, gains_out_ref, white_ref):
+def last_kernel(run, parts_ref, gains_ref, gains_out_ref, white_ref):
     owned = 2 * run
     source = lax.broadcasted_iota(jnp.int32, (run, owned), 0)
     target = lax.broadcasted_iota(jnp.int32, (run, owned), 1)
-    results = stepped(run, at_ref, parts_ref, gains_ref)
+    results = stepped(run, parts_ref, gains_ref)
     for value, out_ref in zip(results, (gains_out_ref, white_ref)):
-        turned = value.T
         out = None
         for odd in range(2):
-            place = jnp.where(target == 2 * source + odd, 1.0, 0.0)
-            part = jnp.dot(
-                turned[odd * VALS : (odd + 1) * VALS],
-                place,
+            part = lax.dot_general(
+                value[:, odd * VALS : (odd + 1) * VALS],
+                jnp.where(target == 2 * source + odd, 1.0, 0.0),
+                (((0,), (0,)), ((), ())),
                 precision=lax.Precision.HIGHEST,
                 preferred_element_type=jnp.float32,
             )
@@ -302,26 +328,26 @@
         out_ref[...] = out
 
 
-def step(run, at, parts, gains):
+def step(run, parts, gains):
     return pl.pallas_call(
         functools.partial(step_kernel, run),
         out_shape=jax.ShapeDtypeStruct(gains.shape, jnp.float32),
-        in_specs=[pl.BlockSpec(memory_space=pltpu.SMEM)] + in_vmem(2),
+        in_specs=in_vmem(2),
         out_specs=in_vmem(1)[0],
         compiler_params=PARAMS,
         name="step",
-    )(at, parts, gains)
-
-
-def last(run, at, parts, gains):
+    )(parts, gains)
+
+
+def last(run, parts, gains):
     return pl.pallas_call(
         functools.partial(last_kernel, run),
         out_shape=(jax.ShapeDtypeStruct((VALS, 2 * run), jnp.float32),) * 2,
-        in_specs=[pl.BlockSpec(memory_space=pltpu.SMEM)] + in_vmem(2),
+        in_specs=in_vmem(2),
         out_specs=tuple(in_vmem(2)),
         compiler_params=PARAMS,
         name="last",
-    )(at, parts, gains)
+    )(parts, gains)
 
 
 def exchange(rows, axes, peers):
@@ -333,27 +359,21 @@
 def per_device(model, vis, weights, antenna1, antenna2, live, gains):
     base = antenna1.shape[0]
     channels = model.shape[1]
-    near, far = ("x", "z0", "core"), ("y", "z1")
-    wide = near + ("z1",)
     first, second, live = (a.reshape(1, base) for a in (antenna1, antenna2, live))
-    data, copies = pack(
-        model.reshape(channels, VALS, base), vis[0], weights[0], live,
+    data, own, copies = pack(
+        model.reshape(channels, VALS, base), vis[0], weights[0], live, first, second,
         gains.reshape(VALS, gains.shape[3]), 32,
     )
     every = lax.all_gather(data, "y")
-    full = exchange(copies, wide, 32)
-
-    at = (lax.axis_index(near) * 16).reshape(1).astype(jnp.int32)
-    sent = partials(16, channels, full, data[None], first, second)
-    sent = total(16, exchange(sent, near, 16), 16)
-    full = exchange(step(16, at, exchange(sent, far, 16), full), near, 16)
-
-    at = (lax.axis_index(wide) * 8).reshape(1).astype(jnp.int32)
+    full = exchange(copies, WIDE, 32)
+    parts = exchange(partials(RUN, channels, full, own[None]), NEAR, 16)
+    sums = exchange(total(RUN, parts, 16), FAR, 16)
+    full = exchange(step(RUN, sums, full), NEAR, 16)
     for turn in range(1, ITERS):
-        sums = exchange(partials(8, channels, full, every, first, second), wide, 32)
+        sums = exchange(partials(RUN // 2, channels, full, every), WIDE, 32)
         if turn < ITERS - 1:
-            full = exchange(step(8, at, sums, full), wide, 32)
-    return tuple(out.reshape(gains.shape) for out in last(8, at, sums, full))
+            full = exchange(step(RUN // 2, sums, full), WIDE, 32)
+    return tuple(out.reshape(gains.shape) for out in last(RUN // 2, sums, full))
 
 
 def solution(mesh):

time: 127 us -> 120 us (0.945)
  blocking collectives: 65.2 us -> 93.7 us
  waiting for transfers between devices: 18.6 us -> 0.02 us
  starting transfers between devices: 11.3 us -> 0.04 us
  local copies, waits for them, and re-layouts: 6.31 us -> 2.21 us
  Pallas kernels: 10.9 us -> 9.52 us
    all_to_all x5 -> x7, blocking collectives: 65.2 us -> 93.7 us  [exchange(): return lax.all_to_all(sent, axes, 0, 0).reshape(count, LANES)]
    all_to_all x2 -> x0, waiting for transfers between devices: 18.6 us -> none  [exchange(): return lax.all_to_all(sent, axes, 0, 0).reshape(count, LANES)]
    all_to_all x2 -> x0, starting transfers between devices: 11.3 us -> none  [exchange(): return lax.all_to_all(sent, axes, 0, 0).reshape(count, LANES)]
    unnamed x22 -> x6, local copies, waits for them, and re-layouts: 6.31 us -> 2.21 us
    pallas_call x3, Pallas kernels: 7.81 us -> 5.84 us  [partials(): pl.pallas_call(functools.partial(partials_kernel, run, channels), out_sha...]
  transfers between devices with their start and end apart: 3 -> 1, of which waited for: 2 -> 0; matrix products, arithmetic and copies ran while one was open for 0% -> 0% of each run, Pallas kernels for 2% -> 1%
where the time goes in v6:
time: 120 us
  blocking collectives  93.7 us (78%)
  between operations  14.1 us (12%)
  Pallas kernels  9.52 us (8%)
  local copies, waits for them, and re-layouts  2.21 us (2%)
    all_to_all x7, blocking collectives, exchange(): return lax.all_to_all(sent, axes, 0, 0).reshape(count, LANES)  93.7 us
    pallas_call x3, Pallas kernels, partials(): pl.pallas_call(functools.partial(partials_kernel, run, channels), out_sha...  5.84 us
  transfers between devices with their start and end apart: 1, of which 0 were waited for; matrix products, arithmetic and copies ran while one was open for 0% of the time, Pallas kernels for 1%

profile of v6, /device:TPU:1, one launch (start us, length us, event | category | flops | bytes accessed | tf_op | source)
XLA Modules:
  0.0 119.6 jit_solution(1835931568358100644)
XLA Ops:
  7.2 0.0 all-gather.3.cloned.1.call-start
  7.2 1.9 %pack.1 = (f32[296,128]{1,0:T(8,128)}, f32[296,128]{1,0:T(8,128)}, f32[256,128]{1,0:T(8,128)}) custom-call(bf16[2,64,256]{2,1,0:T(8,128)(2,1)} %bitcast.45, f32[2,8,256]{2,1,0:T(8,128)} %bitcast.47, f32[2,256]{1,0:T(2,128)} %bitcast.48, s32[1,256]{1,0:T(1,128)} %bitcast.49, s32[1,256]{1,0:T(1,128)} %bitcast.50, s32[1,256]{1,0:T(1,128)} %bitcast.51, ...), custom_call_target="tpu_custom_call" | custom-call | tf_op jit(solution)/shard_map/pack/pallas_call | solution.py:146
  9.1 0.0 all-gather.3.cloned.1.call-update
  9.2 20.1 %all_to_all.35 = f32[32,1,1024]{2,1,0:T(1,128)S(1)} all-to-all(f32[32,1,1024]{2,1,0:T(1,128)} %bitcast.44), channel_id=1, replica_groups=mesh['y'=8,'x'=4,'z1'=2,'z0'=2,'core'=2,'chan'=2] {'x','z0','core','z1'}, dimensions={0} | all-to-all | bytes 262144 | tf_op jit(solution)/shard_map/all_to_all | solution.py:356
  29.2 0.0 copy-start.2
  29.2 0.9 copy-done.2
  30.2 0.9 partials.3
  31.0 9.3 %all_to_all.36 = f32[16,1,2304]{2,1,0:T(1,128)S(1)} all-to-all(f32[16,1,2304]{2,1,0:T(1,128)S(1)} %bitcast.38), channel_id=1, replica_groups=mesh['y'=8,'x'=4,'z1'=2,'z0'=2,'core'=2,'chan'=2] {'x','z0','core'}, dimensions={0} | all-to-all | bytes 294912 | tf_op jit(solution)/shard_map/all_to_all | solution.py:356
  40.3 16.7 %all_to_all.37 = f32[16,1,2304]{2,1,0:T(1,128)S(1)} all-to-all(f32[16,1,2304]{2,1,0:T(1,128)S(1)} %bitcast.40), channel_id=1, replica_groups=mesh['y'=8,'x'=4,'z1'=2,'z0'=2,'core'=2,'chan'=2] {'z1','y'}, dimensions={0} | all-to-all | bytes 294912 | tf_op jit(solution)/shard_map/all_to_all | solution.py:356
  57.0 0.2 step.2
  57.2 11.0 %all_to_all.38 = f32[16,1,2048]{2,1,0:T(1,128)S(1)} all-to-all(f32[16,1,2048]{2,1,0:T(1,128)S(1)} %bitcast.41), channel_id=1, replica_groups=mesh['y'=8,'x'=4,'z1'=2,'z0'=2,'core'=2,'chan'=2] {'x','z0','core'}, dimensions={0} | all-to-all | bytes 262144 | tf_op jit(solution)/shard_map/all_to_all | solution.py:356
  68.3 0.0 all-gather.3.cloned.1.call-done
  68.3 0.0 copy-start
  68.3 1.3 %copy-done = f32[2368,128]{1,0:T(8,128)S(1)} copy-done((f32[2368,128]{1,0:T(8,128)S(1)}, f32[2368,128]{1,0:T(8,128)}, u32[]{:S(2)}) %copy-start) | copy-done | bytes 1212440
  69.5 0.0 copy-start.1
  69.6 2.5 %partials.4 = f32[288,128]{1,0:T(8,128)S(1)} custom-call(f32[256,128]{1,0:T(8,128)S(1)} %bitcast.27, f32[8,296,128]{2,1,0:T(8,128)S(1)} %bitcast.25), custom_call_target="tpu_custom_call" | custom-call | tf_op jit(solution)/shard_map/partials/pallas_call | solution.py:250
  72.1 12.3 %all_to_all.39 = f32[32,1,1152]{2,1,0:T(1,128)S(1)} all-to-all(f32[32,1,1152]{2,1,0:T(1,128)S(1)} %bitcast.34), channel_id=1, replica_groups=mesh['y'=8,'x'=4,'z1'=2,'z0'=2,'core'=2,'chan'=2] {'x','z0','core','z1'}, dimensions={0} | all-to-all | bytes 294912 | tf_op jit(solution)/shard_map/all_to_all | solution.py:356
  84.4 0.2 step.3
  84.6 12.1 %all_to_all.40 = f32[32,1,1024]{2,1,0:T(1,128)S(1)} all-to-all(f32[32,1,1024]{2,1,0:T(1,128)S(1)} %bitcast.42), channel_id=1, replica_groups=mesh['y'=8,'x'=4,'z1'=2,'z0'=2,'core'=2,'chan'=2] {'x','z0','core','z1'}, dimensions={0} | all-to-all | bytes 262144 | tf_op jit(solution)/shard_map/all_to_all | solution.py:356
  96.7 0.0 copy-done.1
  96.7 2.5 %partials.5 = f32[288,128]{1,0:T(8,128)S(1)} custom-call(f32[256,128]{1,0:T(8,128)S(1)} %bitcast.31, f32[8,296,128]{2,1,0:T(8,128)S(1)} %bitcast.26), custom_call_target="tpu_custom_call" | custom-call | tf_op jit(solution)/shard_map/partials/pallas_call | solution.py:250
  99.2 12.3 %all_to_all.41 = f32[32,1,1152]{2,1,0:T(1,128)S(1)} all-to-all(f32[32,1,1152]{2,1,0:T(1,128)S(1)} %bitcast.33), channel_id=1, replica_groups=mesh['y'=8,'x'=4,'z1'=2,'z0'=2,'core'=2,'chan'=2] {'x','z0','core','z1'}, dimensions={0} | all-to-all | bytes 294912 | tf_op jit(solution)/shard_map/all_to_all | solution.py:356
  111.4 1.3 %last.1 = (f32[64,16]{1,0:T(8,128)}, f32[64,16]{1,0:T(8,128)}) custom-call(f32[288,128]{1,0:T(8,128)S(1)} %bitcast.37, f32[256,128]{1,0:T(8,128)S(1)} %bitcast.32), custom_call_target="tpu_custom_call" | custom-call | tf_op jit(solution)/shard_map/last/pallas_call | solution.py:343
  (1 shorter events, 0.0 us)
Async XLA Ops:
  7.2 61.1 %all-gather.3.cloned.1.call-start = ((), (), s32[]{:S(2)}) async-start(), calls=%async_computation.7 | async-start | bytes 1363968 | tf_op jit(solution)/shard_map/all_gather | solution.py:367
  29.2 0.9 copy-start.2
  68.3 1.3 %copy-start = (f32[2368,128]{1,0:T(8,128)S(1)}, f32[2368,128]{1,0:T(8,128)}, u32[]{:S(2)}) copy-start(f32[2368,128]{1,0:T(8,128)} %all-gather.3.cloned.1.call-done) | copy-start | bytes 3637252
  69.5 27.1 %copy-start.1 = (f32[2368,128]{1,0:T(8,128)S(1)}, f32[2368,128]{1,0:T(8,128)}, u32[]{:S(2)}) copy-start(f32[2368,128]{1,0:T(8,128)} %all-gather.3.cloned.1.call-done) | copy-start | bytes 3637252
Sparse Core Ops, SparseCore 0:
  10.1 44.7 all-gather.2

commit v7 on v5

--- a/solution.py
+++ b/solution.py
@@ -177,16 +177,27 @@
 
 
 def total_kernel(parts_ref, copies_ref):
-    rows = RUN + 2
-    total = peers_sum(parts_ref, rows)
-    for at in range(0, copies_ref.shape[0], rows):
-        copies_ref[at : at + rows, :] = total
-
-
-def total(parts, peers):
+    total = peers_sum(parts_ref, RUN + 2)
+    for at in range(0, copies_ref.shape[0], RUN + 2):
+        copies_ref[at : at + RUN + 2, :] = total
+
+
+def total_halves_kernel(parts_ref, copies_ref):
+    total = peers_sum(parts_ref, RUN + 2)
+    run = RUN // 2
+    count = copies_ref.shape[0] // 2
+    for half in range(2):
+        own = jnp.concatenate(
+            [total[half * run : (half + 1) * run], total[RUN + half : RUN + half + 1]], axis=0
+        )
+        for at in range(half * count, (half + 1) * count, run + 1):
+            copies_ref[at : at + run + 1, :] = own
+
+
+def total(parts, peers, kernel, rows):
     return pl.pallas_call(
-        total_kernel,
-        out_shape=jax.ShapeDtypeStruct((peers * (RUN + 2), LANES), jnp.float32),
+        kernel,
+        out_shape=jax.ShapeDtypeStruct((peers * rows, LANES), jnp.float32),
         in_specs=[pl.BlockSpec(memory_space=pltpu.VMEM)],
         out_specs=pl.BlockSpec(memory_space=pltpu.VMEM),
         compiler_params=pltpu.CompilerParams(vmem_limit_bytes=16 * 2**20),
@@ -194,36 +205,38 @@
     )(parts)
 
 
-def stepped(parts_ref, gains_ref):
-    sums = peers_sum(parts_ref, RUN + 2)
-    grad = sums[:RUN]
-    row = lax.broadcasted_iota(jnp.int32, (RUN, LANES), 0)
-    lane = lax.broadcasted_iota(jnp.int32, (RUN, LANES), 1)
-    curv = jnp.where(row < RUN // 2, sums[RUN : RUN + 1], sums[RUN + 1 : RUN + 2])
-    curv = jnp.where(lane // (2 * DIRS) == row % (RUN // 2), curv, 0.0)
+def stepped(run, at, parts_ref, gains_ref):
+    sums = peers_sum(parts_ref, run // 8 * 9)
+    grad = sums[:run]
+    row = lax.broadcasted_iota(jnp.int32, (run, LANES), 0)
+    lane = lax.broadcasted_iota(jnp.int32, (run, LANES), 1)
+    curv = sums[run : run + 1]
+    if run > 8:
+        curv = jnp.where(row < 8, curv, sums[run + 1 : run + 2])
+    curv = jnp.where(lane // (2 * DIRS) == row % 8, curv, 0.0)
     source = lax.broadcasted_iota(jnp.int32, (LANES, LANES), 0)
     target = lax.broadcasted_iota(jnp.int32, (LANES, LANES), 1)
     wide = jnp.where(source % (2 * DIRS) == target // COMPS, 1.0, 0.0)
     denom = 1.0 + jnp.dot(
         curv, wide, precision=lax.Precision.HIGHEST, preferred_element_type=jnp.float32
     )
-    at = lax.axis_index(NEAR) * RUN
-    old = gains_ref[pl.ds(pl.multiple_of(at, RUN), RUN), :]
+    old = gains_ref[pl.ds(pl.multiple_of(at, run), run), :]
     return old - STEP * grad / denom, grad / jnp.sqrt(denom)
 
 
 def step_kernel(parts_ref, gains_ref, copies_ref):
-    gains, _ = stepped(parts_ref, gains_ref)
+    gains, _ = stepped(RUN, lax.axis_index(NEAR) * RUN, parts_ref, gains_ref)
     for at in range(0, copies_ref.shape[0], RUN):
         copies_ref[at : at + RUN, :] = gains
 
 
 def last_kernel(parts_ref, gains_ref, gains_out_ref, white_ref):
     owned = gains_out_ref.shape[1]
-    first = lax.axis_index("z1") * (RUN // 2)
-    source = lax.broadcasted_iota(jnp.int32, (RUN, owned), 0) - first
-    target = lax.broadcasted_iota(jnp.int32, (RUN, owned), 1)
-    results = stepped(parts_ref, gains_ref)
+    run = RUN // 2
+    at = lax.axis_index(NEAR) * RUN + lax.axis_index("z1") * run
+    source = lax.broadcasted_iota(jnp.int32, (run, owned), 0)
+    target = lax.broadcasted_iota(jnp.int32, (run, owned), 1)
+    results = stepped(run, at, parts_ref, gains_ref)
     for value, out_ref in zip(results, (gains_out_ref, white_ref)):
         out = None
         for odd in range(2):
@@ -254,7 +267,7 @@
         last_kernel,
         out_shape=(jax.ShapeDtypeStruct((VALS, owned), jnp.float32),) * 2,
         in_specs=[pl.BlockSpec(memory_space=pltpu.VMEM)] * 2,
-        out_specs=tuple([pl.BlockSpec(memory_space=pltpu.VMEM)] * 2),
+        out_specs=(pl.BlockSpec(memory_space=pltpu.VMEM),) * 2,
         compiler_params=pltpu.CompilerParams(vmem_limit_bytes=16 * 2**20),
         name="last",
     )(parts, gains)
@@ -278,10 +291,12 @@
     full = exchange(mine, NEAR + ("z1",), 32)
     for turn in range(ITERS):
         sent = partials(full, model, vis, weights, live, first, second)
-        sent = total(exchange(sent, NEAR, 16), 16)
-        sums = exchange(sent, FAR, 16)
+        parts = exchange(sent, NEAR, 16)
         if turn < ITERS - 1:
+            sums = exchange(total(parts, 16, total_kernel, RUN + 2), FAR, 16)
             full = exchange(step(sums, full, 16), NEAR, 16)
+        else:
+            sums = exchange(total(parts, 16, total_halves_kernel, RUN // 2 + 1), FAR, 16)
     return tuple(out.reshape(gains.shape) for out in last(sums, full, owned))
 
 

time: 116 us -> 115 us (level)
  no operation moved by 1% of the time
where the time goes in v7:
time: 115 us
  blocking collectives  108 us (94%)
  Pallas kernels  4.36 us (4%)
  local copies, waits for them, and re-layouts  1.68 us (1%)
    all_to_all x9, blocking collectives, exchange(): return lax.all_to_all(sent, axes, 0, 0).reshape(count, LANES)  108 us
    pallas_call x3, Pallas kernels, partials(): pl.pallas_call(partials_kernel, out_shape=jax.ShapeDtypeStruct((pairs //...  2.6 us

profile of v7, /device:TPU:1, one launch (start us, length us, event | category | flops | bytes accessed | tf_op | source)
XLA Modules:
  0.0 114.8 jit_solution(8894361237419639755)
XLA Ops:
  0.6 0.8 copy.10
  1.4 0.1 broadcast_in_dim.7
  1.5 0.1 broadcast_in_dim.8
  1.6 0.0 copy-start
  1.6 0.0 copy-start.1
  1.6 20.0 %all_to_all.45 = f32[32,1,1024]{2,1,0:T(1,128)S(1)} all-to-all(f32[32,1,1024]{2,1,0:T(1,128)S(1)} %broadcast_in_dim.8), channel_id=1, replica_groups=mesh['y'=8,'x'=4,'z1'=2,'z0'=2,'core'=2,'chan'=2] {'x','z0','core','z1'}, dimensions={0} | all-to-all | bytes 262144 | tf_op jit(solution)/shard_map/all_to_all | solution.py:279
  21.6 0.0 copy-start.4
  21.6 0.0 copy-start.5
  21.6 0.0 copy-start.2
  21.6 0.0 copy-start.3
  21.6 0.0 copy-done
  21.6 0.0 copy-done.1
  21.7 0.6 copy-done.4
  22.3 0.0 copy-done.5
  22.3 0.0 copy-done.2
  22.3 0.0 copy-done.3
  22.3 0.9 partials.3
  23.2 9.3 %all_to_all.46 = f32[16,1,2304]{2,1,0:T(1,128)S(1)} all-to-all(f32[16,1,2304]{2,1,0:T(1,128)S(1)} %bitcast.40), channel_id=1, replica_groups=mesh['y'=8,'x'=4,'z1'=2,'z0'=2,'core'=2,'chan'=2] {'x','z0','core'}, dimensions={0} | all-to-all | bytes 294912 | tf_op jit(solution)/shard_map/all_to_all | solution.py:279
  32.6 15.3 %all_to_all.47 = f32[16,1,2304]{2,1,0:T(1,128)S(1)} all-to-all(f32[16,1,2304]{2,1,0:T(1,128)S(1)} %bitcast.36), channel_id=1, replica_groups=mesh['y'=8,'x'=4,'z1'=2,'z0'=2,'core'=2,'chan'=2] {'z1','y'}, dimensions={0} | all-to-all | bytes 294912 | tf_op jit(solution)/shard_map/all_to_all | solution.py:279
  47.8 0.2 step.2
  48.0 10.9 %all_to_all.48 = f32[16,1,2048]{2,1,0:T(1,128)S(1)} all-to-all(f32[16,1,2048]{2,1,0:T(1,128)S(1)} %bitcast.46), channel_id=1, replica_groups=mesh['y'=8,'x'=4,'z1'=2,'z0'=2,'core'=2,'chan'=2] {'x','z0','core'}, dimensions={0} | all-to-all | bytes 262144 | tf_op jit(solution)/shard_map/all_to_all | solution.py:279
  59.0 0.9 partials.4
  59.8 9.4 %all_to_all.49 = f32[16,1,2304]{2,1,0:T(1,128)S(1)} all-to-all(f32[16,1,2304]{2,1,0:T(1,128)S(1)} %bitcast.41), channel_id=1, replica_groups=mesh['y'=8,'x'=4,'z1'=2,'z0'=2,'core'=2,'chan'=2] {'x','z0','core'}, dimensions={0} | all-to-all | bytes 294912 | tf_op jit(solution)/shard_map/all_to_all | solution.py:279
  69.3 11.3 %all_to_all.50 = f32[16,1,2304]{2,1,0:T(1,128)S(1)} all-to-all(f32[16,1,2304]{2,1,0:T(1,128)S(1)} %bitcast.38), channel_id=1, replica_groups=mesh['y'=8,'x'=4,'z1'=2,'z0'=2,'core'=2,'chan'=2] {'z1','y'}, dimensions={0} | all-to-all | bytes 294912 | tf_op jit(solution)/shard_map/all_to_all | solution.py:279
  80.7 0.2 step.3
  80.9 10.9 %all_to_all.51 = f32[16,1,2048]{2,1,0:T(1,128)S(1)} all-to-all(f32[16,1,2048]{2,1,0:T(1,128)S(1)} %bitcast.47), channel_id=1, replica_groups=mesh['y'=8,'x'=4,'z1'=2,'z0'=2,'core'=2,'chan'=2] {'x','z0','core'}, dimensions={0} | all-to-all | bytes 262144 | tf_op jit(solution)/shard_map/all_to_all | solution.py:279
  91.8 0.9 partials.5
  92.7 9.4 %all_to_all.52 = f32[16,1,2304]{2,1,0:T(1,128)S(1)} all-to-all(f32[16,1,2304]{2,1,0:T(1,128)S(1)} %bitcast.42), channel_id=1, replica_groups=mesh['y'=8,'x'=4,'z1'=2,'z0'=2,'core'=2,'chan'=2] {'x','z0','core'}, dimensions={0} | all-to-all | bytes 294912 | tf_op jit(solution)/shard_map/all_to_all | solution.py:279
  102.1 11.4 %all_to_all.53 = f32[16,1,1152]{2,1,0:T(1,128)S(1)} all-to-all(f32[16,1,1152]{2,1,0:T(1,128)S(1)} %bitcast.49), channel_id=1, replica_groups=mesh['y'=8,'x'=4,'z1'=2,'z0'=2,'core'=2,'chan'=2] {'z1','y'}, dimensions={0} | all-to-all | bytes 147456 | tf_op jit(solution)/shard_map/all_to_all | solution.py:279
  113.5 1.3 %last.1 = (f32[64,16]{1,0:T(8,128)}, f32[64,16]{1,0:T(8,128)}) custom-call(f32[144,128]{1,0:T(8,128)S(1)} %bitcast.48, f32[256,128]{1,0:T(8,128)S(1)} %bitcast.32), custom_call_target="tpu_custom_call" | custom-call | tf_op jit(solution)/shard_map/last/pallas_call | solution.py:266
  (3 shorter events, 0.1 us)
Async XLA Ops:
  1.6 20.0 %copy-start = (bf16[1,2,8,8,256]{4,3,2,1,0:T(8,128)(2,1)S(1)}, bf16[1,2,8,8,256]{4,3,2,1,0:T(8,128)(2,1)}, u32[]{:S(2)}) copy-start(bf16[1,2,8,8,256]{4,3,2,1,0:T(8,128)(2,1)} %param.7) | copy-start | bytes 196612
  1.6 20.0 %copy-start.1 = (f32[1,2,8,256]{3,2,1,0:T(8,128)S(1)}, f32[1,2,8,256]{3,2,1,0:T(8,128)}, u32[]{:S(2)}) copy-start(f32[1,2,8,256]{3,2,1,0:T(8,128)} %param.8) | copy-start | bytes 49156
  21.6 0.7 copy-start.4
  21.6 0.7 copy-start.5
  21.6 0.7 copy-start.2
  21.6 0.7 copy-start.3

commit v8 on v7

--- a/solution.py
+++ b/solution.py
@@ -74,21 +74,76 @@
     return kept | ((station & 0b110000) << 1) | ((station >> 2) & 0b10000)
 
 
+def open_kernel(*refs):
+    sources, (copies_ref, rows_ref), targets, sems = refs[:5], refs[5:7], refs[7:12], refs[12]
+    moves = [
+        pltpu.make_async_copy(source, target, sems.at[index])
+        for index, (source, target) in enumerate(zip(sources, targets))
+    ]
+    for move in moves:
+        move.start()
+    for move in moves:
+        move.wait()
+    gains_ref, weight_ref, live_ref, first_ref, second_ref = targets
+    owned = gains_ref.shape[1]
+    target = lax.broadcasted_iota(jnp.int32, (owned // 2, owned), 0)
+    source = lax.broadcasted_iota(jnp.int32, (owned // 2, owned), 1)
+    mine = jnp.concatenate(
+        [
+            lax.dot_general(
+                jnp.where(source == 2 * target + odd, 1.0, 0.0),
+                gains_ref[...],
+                (((1,), (1,)), ((), ())),
+                precision=lax.Precision.HIGHEST,
+                preferred_element_type=jnp.float32,
+            )
+            for odd in range(2)
+        ],
+        axis=1,
+    )
+    for at in range(0, copies_ref.shape[0], owned // 2):
+        copies_ref[at : at + owned // 2, :] = mine
+    live = live_ref[...].astype(jnp.float32)
+    lines = [weight_ref[c : c + 1, :] * live for c in range(weight_ref.shape[0])]
+    lines += [first_ref[...].astype(jnp.float32), second_ref[...].astype(jnp.float32)]
+    cuts = live.shape[1] // LANES
+    rows_ref[...] = jnp.concatenate(
+        [line[:, cut * LANES : (cut + 1) * LANES] for line in lines for cut in range(cuts)], axis=0
+    )
+
+
+def opened(peers, *args):
+    gains, weights = args[:2]
+    channels, base = weights.shape
+    return pl.pallas_call(
+        open_kernel,
+        out_shape=(
+            jax.ShapeDtypeStruct((peers * gains.shape[1] // 2, LANES), jnp.float32),
+            jax.ShapeDtypeStruct(((channels + 2) * base // LANES, LANES), jnp.float32),
+        ),
+        in_specs=[pl.BlockSpec(memory_space=pltpu.HBM)] * 5,
+        out_specs=(pl.BlockSpec(memory_space=pltpu.VMEM),) * 2,
+        scratch_shapes=[pltpu.VMEM(a.shape, a.dtype) for a in args]
+        + [pltpu.SemaphoreType.DMA((5,))],
+        compiler_params=pltpu.CompilerParams(vmem_limit_bytes=16 * 2**20),
+        name="opened",
+    )(*(pltpu.with_memory_space_constraint(a, pltpu.HBM) for a in args))
+
+
 def partials_kernel(
-    gains_ref, model_ref, vis_ref, weight_ref, live_ref, first_ref, second_ref,
-    out_ref, picked_ref, model_f_ref, terms_ref,
+    gains_ref, model_ref, vis_ref, rows_ref, out_ref, picked_ref, model_f_ref, terms_ref
 ):
-    base = first_ref.shape[1]
     pairs = gains_ref.shape[0]
-    channels = model_ref.shape[0]
-    station = placed(jnp.concatenate([first_ref[...], second_ref[...]], axis=1))
+    channels, _, base = model_ref.shape
+    cuts = base // LANES
+    ends = [rows_ref[channels * cuts + i : channels * cuts + i + 1, :] for i in range(2 * cuts)]
+    station = placed(jnp.concatenate(ends, axis=1).astype(jnp.int32))
     rows = lax.broadcasted_iota(jnp.int32, (pairs, 2 * base), 0)
     hot = jnp.where(rows == station // 2, 1.0, 0.0).astype(jnp.bfloat16)
     odd = station % 2 == 1
 
     both = select_sum(gains_ref[...].T, hot, ((1,), (0,)))
     picked = jnp.where(odd, both[VALS:], both[:VALS])
-    cuts = base // LANES
     for cut in range(2 * cuts):
         picked_ref[cut] = picked[:, cut * LANES : (cut + 1) * LANES]
 
@@ -96,7 +151,6 @@
         comps = [ref[at, pl.ds(c, DIRS, stride=COMPS), :] for c in range(COMPS)]
         return [(comps[i], comps[i + 4]) for i in range(4)]
 
-    live = live_ref[...].astype(jnp.float32)
     curvs = [None] * (2 * cuts)
     for cut in range(cuts):
         lanes = slice(cut * LANES, (cut + 1) * LANES)
@@ -106,7 +160,8 @@
         for channel in range(channels):
             model_f_ref[0] = model_ref[channel, :, lanes].astype(jnp.float32)
             model = entries(model_f_ref, 0)
-            scale = weight_ref[channel : channel + 1, lanes] * live[:, lanes]
+            part = channel * cuts + cut
+            scale = rows_ref[part : part + 1, :]
             right_a = product(model, adjoint(far))
             left_b = product(near, model)
             each = product(near, right_a)
@@ -151,13 +206,13 @@
         out_ref[at + RUN : at + RUN + 2, :] = curvs[2 * peer : 2 * peer + 2]
 
 
-def partials(gains, model, vis, weights, live, first, second):
+def partials(gains, model, vis, rows):
     pairs = gains.shape[0]
-    base = first.shape[1]
+    base = model.shape[2]
     return pl.pallas_call(
         partials_kernel,
         out_shape=jax.ShapeDtypeStruct((pairs // RUN * (RUN + 2), LANES), jnp.float32),
-        in_specs=[pl.BlockSpec(memory_space=pltpu.VMEM)] * 7,
+        in_specs=[pl.BlockSpec(memory_space=pltpu.VMEM)] * 4,
         out_specs=pl.BlockSpec(memory_space=pltpu.VMEM),
         scratch_shapes=[
             pltpu.VMEM((2 * base // LANES, VALS, LANES), jnp.float32),
@@ -166,7 +221,7 @@
         ],
         compiler_params=pltpu.CompilerParams(vmem_limit_bytes=16 * 2**20),
         name="partials",
-    )(gains, model, vis, weights, live, first, second)
+    )(gains, model, vis, rows)
 
 
 def peers_sum(parts_ref, rows):
@@ -286,11 +341,10 @@
     model = model.reshape(channels, VALS, base)
     vis, weights = vis[0], weights[0]
     first, second, live = (a.reshape(1, base) for a in (antenna1, antenna2, live))
-    mine = gains.reshape(VALS, owned).T.reshape(1, owned * VALS // LANES, LANES)
-    mine = jnp.broadcast_to(mine, (32,) + mine.shape[1:]).reshape(-1, LANES)
-    full = exchange(mine, NEAR + ("z1",), 32)
+    copies, rows = opened(32, gains.reshape(VALS, owned), weights, live, first, second)
+    full = exchange(copies, NEAR + ("z1",), 32)
     for turn in range(ITERS):
-        sent = partials(full, model, vis, weights, live, first, second)
+        sent = partials(full, model, vis, rows)
         parts = exchange(sent, NEAR, 16)
         if turn < ITERS - 1:
             sums = exchange(total(parts, 16, total_kernel, RUN + 2), FAR, 16)

time: 115 us -> 115 us (level)
  local copies, waits for them, and re-layouts: 1.68 us -> 0.01 us
where the time goes in v8:
time: 115 us; the launch traced here: 114 us
  blocking collectives  108 us (94%)
  Pallas kernels  5.43 us (5%)
    all_to_all x9, blocking collectives, exchange(): return lax.all_to_all(sent, axes, 0, 0).reshape(count, LANES)  108 us
    pallas_call x3, Pallas kernels, partials(): pl.pallas_call(partials_kernel, out_shape=jax.ShapeDtypeStruct((pairs //...  2.57 us

profile of v8, /device:TPU:1, one launch (start us, length us, event | category | flops | bytes accessed | tf_op | source)
XLA Modules:
  0.0 114.2 jit_solution(4050162599391451322)
XLA Ops:
  0.6 1.1 opened.1
  1.7 0.0 copy-start
  1.8 0.0 copy-start.1
  1.8 20.0 %all_to_all.45 = f32[32,1,1024]{2,1,0:T(1,128)S(1)} all-to-all(f32[32,1,1024]{2,1,0:T(1,128)S(1)} %bitcast.53), channel_id=1, replica_groups=mesh['y'=8,'x'=4,'z1'=2,'z0'=2,'core'=2,'chan'=2] {'x','z0','core','z1'}, dimensions={0} | all-to-all | bytes 262144 | tf_op jit(solution)/shard_map/all_to_all | solution.py:334
  21.8 0.0 copy-done
  21.8 0.0 copy-done.1
  21.8 0.9 partials.3
  22.6 9.3 %all_to_all.46 = f32[16,1,2304]{2,1,0:T(1,128)S(1)} all-to-all(f32[16,1,2304]{2,1,0:T(1,128)S(1)} %bitcast.41), channel_id=1, replica_groups=mesh['y'=8,'x'=4,'z1'=2,'z0'=2,'core'=2,'chan'=2] {'x','z0','core'}, dimensions={0} | all-to-all | bytes 294912 | tf_op jit(solution)/shard_map/all_to_all | solution.py:334
  32.0 15.3 %all_to_all.47 = f32[16,1,2304]{2,1,0:T(1,128)S(1)} all-to-all(f32[16,1,2304]{2,1,0:T(1,128)S(1)} %bitcast.36), channel_id=1, replica_groups=mesh['y'=8,'x'=4,'z1'=2,'z0'=2,'core'=2,'chan'=2] {'z1','y'}, dimensions={0} | all-to-all | bytes 294912 | tf_op jit(solution)/shard_map/all_to_all | solution.py:334
  47.2 0.2 step.2
  47.4 10.9 %all_to_all.48 = f32[16,1,2048]{2,1,0:T(1,128)S(1)} all-to-all(f32[16,1,2048]{2,1,0:T(1,128)S(1)} %bitcast.46), channel_id=1, replica_groups=mesh['y'=8,'x'=4,'z1'=2,'z0'=2,'core'=2,'chan'=2] {'x','z0','core'}, dimensions={0} | all-to-all | bytes 262144 | tf_op jit(solution)/shard_map/all_to_all | solution.py:334
  58.4 0.9 partials.4
  59.2 9.4 %all_to_all.49 = f32[16,1,2304]{2,1,0:T(1,128)S(1)} all-to-all(f32[16,1,2304]{2,1,0:T(1,128)S(1)} %bitcast.42), channel_id=1, replica_groups=mesh['y'=8,'x'=4,'z1'=2,'z0'=2,'core'=2,'chan'=2] {'x','z0','core'}, dimensions={0} | all-to-all | bytes 294912 | tf_op jit(solution)/shard_map/all_to_all | solution.py:334
  68.7 11.3 %all_to_all.50 = f32[16,1,2304]{2,1,0:T(1,128)S(1)} all-to-all(f32[16,1,2304]{2,1,0:T(1,128)S(1)} %bitcast.38), channel_id=1, replica_groups=mesh['y'=8,'x'=4,'z1'=2,'z0'=2,'core'=2,'chan'=2] {'z1','y'}, dimensions={0} | all-to-all | bytes 294912 | tf_op jit(solution)/shard_map/all_to_all | solution.py:334
  80.0 0.2 step.3
  80.2 10.9 %all_to_all.51 = f32[16,1,2048]{2,1,0:T(1,128)S(1)} all-to-all(f32[16,1,2048]{2,1,0:T(1,128)S(1)} %bitcast.47), channel_id=1, replica_groups=mesh['y'=8,'x'=4,'z1'=2,'z0'=2,'core'=2,'chan'=2] {'x','z0','core'}, dimensions={0} | all-to-all | bytes 262144 | tf_op jit(solution)/shard_map/all_to_all | solution.py:334
  91.2 0.9 partials.5
  92.0 9.4 %all_to_all.52 = f32[16,1,2304]{2,1,0:T(1,128)S(1)} all-to-all(f32[16,1,2304]{2,1,0:T(1,128)S(1)} %bitcast.39), channel_id=1, replica_groups=mesh['y'=8,'x'=4,'z1'=2,'z0'=2,'core'=2,'chan'=2] {'x','z0','core'}, dimensions={0} | all-to-all | bytes 294912 | tf_op jit(solution)/shard_map/all_to_all | solution.py:334
  101.5 11.4 %all_to_all.53 = f32[16,1,1152]{2,1,0:T(1,128)S(1)} all-to-all(f32[16,1,1152]{2,1,0:T(1,128)S(1)} %bitcast.49), channel_id=1, replica_groups=mesh['y'=8,'x'=4,'z1'=2,'z0'=2,'core'=2,'chan'=2] {'z1','y'}, dimensions={0} | all-to-all | bytes 147456 | tf_op jit(solution)/shard_map/all_to_all | solution.py:334
  112.9 1.3 %last.1 = (f32[64,16]{1,0:T(8,128)}, f32[64,16]{1,0:T(8,128)}) custom-call(f32[144,128]{1,0:T(8,128)S(1)} %bitcast.48, f32[256,128]{1,0:T(8,128)S(1)} %bitcast.32), custom_call_target="tpu_custom_call" | custom-call | tf_op jit(solution)/shard_map/last/pallas_call | solution.py:321
  (3 shorter events, 0.1 us)
Async XLA Ops:
  1.7 20.0 %copy-start = (bf16[1,2,8,8,256]{4,3,2,1,0:T(8,128)(2,1)S(1)}, bf16[1,2,8,8,256]{4,3,2,1,0:T(8,128)(2,1)}, u32[]{:S(2)}) copy-start(bf16[1,2,8,8,256]{4,3,2,1,0:T(8,128)(2,1)} %param.7) | copy-start | bytes 196612
  1.8 20.0 %copy-start.1 = (f32[1,2,8,256]{3,2,1,0:T(8,128)S(1)}, f32[1,2,8,256]{3,2,1,0:T(8,128)}, u32[]{:S(2)}) copy-start(f32[1,2,8,256]{3,2,1,0:T(8,128)} %param.8) | copy-start | bytes 49156

commit v9 on v8

--- a/solution.py
+++ b/solution.py
@@ -285,14 +285,18 @@
         copies_ref[at : at + RUN, :] = gains
 
 
-def last_kernel(parts_ref, gains_ref, gains_out_ref, white_ref):
+def last_kernel(parts_ref, gains_ref, gains_hbm, white_hbm, gains_out_ref, white_ref, sems):
     owned = gains_out_ref.shape[1]
     run = RUN // 2
     at = lax.axis_index(NEAR) * RUN + lax.axis_index("z1") * run
     source = lax.broadcasted_iota(jnp.int32, (run, owned), 0)
     target = lax.broadcasted_iota(jnp.int32, (run, owned), 1)
     results = stepped(run, at, parts_ref, gains_ref)
-    for value, out_ref in zip(results, (gains_out_ref, white_ref)):
+    moves = [
+        pltpu.make_async_copy(gains_out_ref, gains_hbm, sems.at[0]),
+        pltpu.make_async_copy(white_ref, white_hbm, sems.at[1]),
+    ]
+    for value, out_ref, move in zip(results, (gains_out_ref, white_ref), moves):
         out = None
         for odd in range(2):
             part = lax.dot_general(
@@ -304,6 +308,9 @@
             )
             out = part if out is None else out + part
         out_ref[...] = out
+        move.start()
+    for move in moves:
+        move.wait()
 
 
 def step(parts, gains, peers):
@@ -322,7 +329,9 @@
         last_kernel,
         out_shape=(jax.ShapeDtypeStruct((VALS, owned), jnp.float32),) * 2,
         in_specs=[pl.BlockSpec(memory_space=pltpu.VMEM)] * 2,
-        out_specs=(pl.BlockSpec(memory_space=pltpu.VMEM),) * 2,
+        out_specs=(pl.BlockSpec(memory_space=pltpu.HBM),) * 2,
+        scratch_shapes=[pltpu.VMEM((VALS, owned), jnp.float32)] * 2
+        + [pltpu.SemaphoreType.DMA((2,))],
         compiler_params=pltpu.CompilerParams(vmem_limit_bytes=16 * 2**20),
         name="last",
     )(parts, gains)

time: 115 us -> 115 us (level)
  no operation moved by 1% of the time
where the time goes in v9:
time: 115 us; the launch traced here: 114 us
  blocking collectives  108 us (94%)
  Pallas kernels  5.46 us (5%)
    all_to_all x9, blocking collectives, exchange(): return lax.all_to_all(sent, axes, 0, 0).reshape(count, LANES)  108 us
    pallas_call x3, Pallas kernels, partials(): pl.pallas_call(partials_kernel, out_shape=jax.ShapeDtypeStruct((pairs //...  2.57 us

profile of v9, /device:TPU:1, one launch (start us, length us, event | category | flops | bytes accessed | tf_op | source)
XLA Modules:
  0.0 114.2 jit_solution(144097503080054650)
XLA Ops:
  0.6 1.1 opened.1
  1.7 0.0 copy-start
  1.8 0.0 copy-start.1
  1.8 20.0 %all_to_all.45 = f32[32,1,1024]{2,1,0:T(1,128)S(1)} all-to-all(f32[32,1,1024]{2,1,0:T(1,128)S(1)} %bitcast.53), channel_id=1, replica_groups=mesh['y'=8,'x'=4,'z1'=2,'z0'=2,'core'=2,'chan'=2] {'x','z0','core','z1'}, dimensions={0} | all-to-all | bytes 262144 | tf_op jit(solution)/shard_map/all_to_all | solution.py:343
  21.8 0.0 copy-done
  21.8 0.0 copy-done.1
  21.8 0.9 partials.3
  22.6 9.3 %all_to_all.46 = f32[16,1,2304]{2,1,0:T(1,128)S(1)} all-to-all(f32[16,1,2304]{2,1,0:T(1,128)S(1)} %bitcast.41), channel_id=1, replica_groups=mesh['y'=8,'x'=4,'z1'=2,'z0'=2,'core'=2,'chan'=2] {'x','z0','core'}, dimensions={0} | all-to-all | bytes 294912 | tf_op jit(solution)/shard_map/all_to_all | solution.py:343
  32.0 15.3 %all_to_all.47 = f32[16,1,2304]{2,1,0:T(1,128)S(1)} all-to-all(f32[16,1,2304]{2,1,0:T(1,128)S(1)} %bitcast.36), channel_id=1, replica_groups=mesh['y'=8,'x'=4,'z1'=2,'z0'=2,'core'=2,'chan'=2] {'z1','y'}, dimensions={0} | all-to-all | bytes 294912 | tf_op jit(solution)/shard_map/all_to_all | solution.py:343
  47.2 0.2 step.2
  47.4 10.9 %all_to_all.48 = f32[16,1,2048]{2,1,0:T(1,128)S(1)} all-to-all(f32[16,1,2048]{2,1,0:T(1,128)S(1)} %bitcast.46), channel_id=1, replica_groups=mesh['y'=8,'x'=4,'z1'=2,'z0'=2,'core'=2,'chan'=2] {'x','z0','core'}, dimensions={0} | all-to-all | bytes 262144 | tf_op jit(solution)/shard_map/all_to_all | solution.py:343
  58.4 0.9 partials.4
  59.2 9.4 %all_to_all.49 = f32[16,1,2304]{2,1,0:T(1,128)S(1)} all-to-all(f32[16,1,2304]{2,1,0:T(1,128)S(1)} %bitcast.42), channel_id=1, replica_groups=mesh['y'=8,'x'=4,'z1'=2,'z0'=2,'core'=2,'chan'=2] {'x','z0','core'}, dimensions={0} | all-to-all | bytes 294912 | tf_op jit(solution)/shard_map/all_to_all | solution.py:343
  68.7 11.3 %all_to_all.50 = f32[16,1,2304]{2,1,0:T(1,128)S(1)} all-to-all(f32[16,1,2304]{2,1,0:T(1,128)S(1)} %bitcast.38), channel_id=1, replica_groups=mesh['y'=8,'x'=4,'z1'=2,'z0'=2,'core'=2,'chan'=2] {'z1','y'}, dimensions={0} | all-to-all | bytes 294912 | tf_op jit(solution)/shard_map/all_to_all | solution.py:343
  80.0 0.2 step.3
  80.2 10.9 %all_to_all.51 = f32[16,1,2048]{2,1,0:T(1,128)S(1)} all-to-all(f32[16,1,2048]{2,1,0:T(1,128)S(1)} %bitcast.47), channel_id=1, replica_groups=mesh['y'=8,'x'=4,'z1'=2,'z0'=2,'core'=2,'chan'=2] {'x','z0','core'}, dimensions={0} | all-to-all | bytes 262144 | tf_op jit(solution)/shard_map/all_to_all | solution.py:343
  91.2 0.9 partials.5
  92.0 9.4 %all_to_all.52 = f32[16,1,2304]{2,1,0:T(1,128)S(1)} all-to-all(f32[16,1,2304]{2,1,0:T(1,128)S(1)} %bitcast.39), channel_id=1, replica_groups=mesh['y'=8,'x'=4,'z1'=2,'z0'=2,'core'=2,'chan'=2] {'x','z0','core'}, dimensions={0} | all-to-all | bytes 294912 | tf_op jit(solution)/shard_map/all_to_all | solution.py:343
  101.5 11.4 %all_to_all.53 = f32[16,1,1152]{2,1,0:T(1,128)S(1)} all-to-all(f32[16,1,1152]{2,1,0:T(1,128)S(1)} %bitcast.49), channel_id=1, replica_groups=mesh['y'=8,'x'=4,'z1'=2,'z0'=2,'core'=2,'chan'=2] {'z1','y'}, dimensions={0} | all-to-all | bytes 147456 | tf_op jit(solution)/shard_map/all_to_all | solution.py:343
  112.9 1.3 %last.1 = (f32[64,16]{1,0:T(8,128)}, f32[64,16]{1,0:T(8,128)}) custom-call(f32[144,128]{1,0:T(8,128)S(1)} %bitcast.48, f32[256,128]{1,0:T(8,128)S(1)} %bitcast.32), custom_call_target="tpu_custom_call" | custom-call | tf_op jit(solution)/shard_map/last/pallas_call | solution.py:328
  (3 shorter events, 0.1 us)
Async XLA Ops:
  1.7 20.0 %copy-start = (bf16[1,2,8,8,256]{4,3,2,1,0:T(8,128)(2,1)S(1)}, bf16[1,2,8,8,256]{4,3,2,1,0:T(8,128)(2,1)}, u32[]{:S(2)}) copy-start(bf16[1,2,8,8,256]{4,3,2,1,0:T(8,128)(2,1)} %param.7) | copy-start | bytes 196612
  1.8 20.0 %copy-start.1 = (f32[1,2,8,256]{3,2,1,0:T(8,128)S(1)}, f32[1,2,8,256]{3,2,1,0:T(8,128)}, u32[]{:S(2)}) copy-start(f32[1,2,8,256]{3,2,1,0:T(8,128)} %param.8) | copy-start | bytes 49156
